TPU v7x, 512 devices: a whole 4x4x16 slice. The times are simulated.
512 devices in a mesh: gx: 4 (over z_hi), gy: 8 (over y, core), gz: 16 (over x, z_lo).
Axes of the slice: x: 4, y: 4, z: 16 (z_hi: 4, z_lo: 4; z = z_hi * 4 + z_lo), core: 2. Of those that a mesh axis runs over, the one named last changes fastest.
Arguments:
- right_side: float32 [64, 256, 2048], P('gx', 'gy', 'gz'), may hold values from -64 to 64
- coefficient: float32 [64, 256, 2048], P('gx', 'gy', 'gz'), may hold values from 0.1 to 10
Outputs:
- solution_field: float32 [64, 256, 2048], P('gx', 'gy', 'gz')
- residual: float32 [64, 256, 2048], P('gx', 'gy', 'gz')
All inputs are finite; a program needn't handle non-finite values.
Results may differ from a plain program's by a relative error of at most 0.02.
Values sent between devices are 32-bit elements; how exact they have to be, the bound alone decides.
A program may use at most 64 MiB of HBM per device.

v0:
```python
from functools import partial
import functools

import jax
import jax.numpy as jnp
import numpy as np
from jax import lax
from jax.sharding import PartitionSpec as P

ORDER = 7
ITERS = 2


HIGHEST_MODE = lax.Precision.HIGHEST


def extended(cells, sides, width):
    for axis, dim in sides:
        count = lax.axis_size(axis)
        ends = count - 1
        head = lax.slice_in_dim(cells, 0, width, axis=dim)
        tail = lax.slice_in_dim(cells, cells.shape[dim] - width, cells.shape[dim], axis=dim)
        cells = jnp.concatenate(
            [
                lax.ppermute(tail, axis, [(i, (i + 1) % count) for i in range(ends)]),
                cells,
                lax.ppermute(head, axis, [((i + 1) % count, i) for i in range(ends)]),
            ],
            axis=dim,
        )
    return cells


def legendre_rows(points, degree):
    table_rows = [np.ones(points.shape), points * 1.0]
    for k in range(2, degree + 1):
        table_rows.append(
            ((2 * k - 1) * points * table_rows[k - 1] - (k - 1) * table_rows[k - 2]) / k
        )
    return table_rows


def lobatto_tables(degree):
    per_side = degree + 1
    points = np.cos(np.pi * np.arange(per_side) / degree)
    for newton_step in range(60):
        table_rows = legendre_rows(points, degree)
        points = points - (points * table_rows[degree] - table_rows[degree - 1]) / (
            per_side * table_rows[degree]
        )
    top_row = legendre_rows(points, degree)[degree][::-1]
    points = points[::-1]
    weights = 2.0 / (degree * per_side * top_row**2)
    deriv_np = np.zeros((per_side, per_side))
    for a in range(per_side):
        for b in range(per_side):
            if a != b:
                deriv_np[a, b] = top_row[a] / (top_row[b] * (points[a] - points[b]))
    deriv_np[0, 0] = -degree * per_side / 4.0
    deriv_np[-1, -1] = degree * per_side / 4.0
    return (weights, deriv_np)


def sine_tables(degree):
    box_side = degree + 3
    grid_index = np.arange(1, box_side + 1)
    sine_np = np.sqrt(2.0 / (box_side + 1)) * np.sin(
        np.pi * np.outer(grid_index, grid_index) / (box_side + 1)
    )
    eigen_values = 2.0 - 2.0 * np.cos(np.pi * grid_index / (box_side + 1))
    summed = eigen_values[:, None, None] + eigen_values[None, :, None] + eigen_values[None, None, :]
    return (sine_np, 1.0 / summed)


def along(function, field, axis):
    if axis == 0:
        return function(field)
    return jax.vmap(functools.partial(along, function, axis=axis - 1))(field)


def pad_first(field, lower, upper):
    return jnp.pad(field, [(lower, upper)] + [(0, 0)] * (field.ndim - 1))


def assemble_first(field, offset, per_side):
    length = field.shape[0]
    local_index = (np.arange(length) - offset) % per_side
    bcast_shape = (length,) + (1,) * (field.ndim - 1)
    at_start = jnp.asarray((local_index == 0).reshape(bcast_shape), jnp.float32)
    at_end = jnp.asarray((local_index == per_side - 1).reshape(bcast_shape), jnp.float32)
    before = pad_first(field[:-1], 1, 0)
    after = pad_first(field[1:], 0, 1)
    return field + at_start * before + at_end * after


def fold_first(field):
    extent = field.shape[0] - 8
    center = field[4 : extent + 4]
    return (
        center
        + pad_first(field[0:2], 0, extent - 2)
        + pad_first(field[extent + 6 :], extent - 2, 0)
    )


def gather_boxes_first(field, per_side):
    elements = (field.shape[0] - 4) // per_side
    trailing = field.shape[1:]
    own_part = field[2 : 2 + per_side * elements].reshape((elements, per_side) + trailing)
    left_part = field[0 : per_side * elements : per_side][:, None]
    right_part = field[per_side + 3 : per_side * elements + 4 : per_side][:, None]
    joined = jnp.concatenate([left_part, own_part, right_part], axis=1)
    return joined.reshape((elements * (per_side + 2),) + trailing)


def scatter_boxes_first(boxes, per_side):
    elements = boxes.shape[0] // (per_side + 2)
    trailing = boxes.shape[1:]
    shaped = boxes.reshape((elements, per_side + 2) + trailing)
    extent = elements * per_side
    own_part = shaped[:, 1 : per_side + 1].reshape((extent,) + trailing)
    zero_slot = jnp.zeros_like(shaped[:, :1])
    left_part = jnp.concatenate([shaped[:, :1]] + [zero_slot] * (per_side - 1), axis=1).reshape(
        (extent,) + trailing
    )
    right_part = jnp.concatenate(
        [zero_slot] * 3 + [shaped[:, -1:]] + [zero_slot] * (per_side - 4), axis=1
    ).reshape((extent,) + trailing)
    return (
        pad_first(own_part, 2, 2)
        + pad_first(left_part, 0, 4)
        + pad_first(right_part, per_side, 0)[: extent + 4]
    )


def contract_first(matrix, field, per_side):
    shaped = field.reshape((field.shape[0] // per_side, per_side) + field.shape[1:])
    product = jnp.einsum("ij,aj...->ai...", matrix, shaped, precision=HIGHEST_MODE)
    return product.reshape((-1,) + field.shape[1:])


def edge_weights(extent, per_side, at_first, at_last):
    position = jnp.arange(extent)
    local_index = position % per_side
    vector = jnp.where((local_index == 0) | (local_index == per_side - 1), 0.5, 1.0)
    vector = jnp.where((position == 0) & at_first, 1.0, vector)
    vector = jnp.where((position == extent - 1) & at_last, 1.0, vector)
    return vector.astype(jnp.float32)


def assemble_seams(field, per_side):
    padded = extended(field, (("gx", 0), ("gy", 1), ("gz", 2)), 1)
    for dim_id in range(3):
        padded = along(partial(assemble_first, offset=1, per_side=per_side), padded, dim_id)
    return padded[1:-1, 1:-1, 1:-1]


def stiffness(field, weighted, deriv_mat, kron_deriv):
    per_side = deriv_mat.shape[0]
    gradient = jnp.matmul(field, kron_deriv.T, precision=HIGHEST_MODE)
    summed = jnp.matmul(weighted * gradient, kron_deriv, precision=HIGHEST_MODE)
    for dim_id in (0, 1):
        gradient = along(partial(contract_first, deriv_mat, per_side=per_side), field, dim_id)
        summed = summed + along(
            partial(contract_first, deriv_mat.T, per_side=per_side), weighted * gradient, dim_id
        )
    return summed


def shards(right_side, coefficient):
    per_side = ORDER + 1
    box_side = ORDER + 3
    span_x, span_y, span_z = right_side.shape
    elem_x = span_x // per_side
    elem_y = span_y // per_side
    elem_z = span_z // per_side
    weights, deriv_np = lobatto_tables(ORDER)
    sine_np, inverse = sine_tables(ORDER)
    deriv_mat = jnp.asarray(deriv_np, jnp.float32)
    kron_deriv = jnp.asarray(np.kron(np.eye(elem_z), deriv_np), jnp.float32)
    sine_basis = jnp.asarray(sine_np, jnp.float32)
    selector = np.zeros((span_z + 4, elem_z * box_side))
    for e in range(elem_z):
        selector[per_side * e, e * box_side] = 1.0
        for b in range(per_side):
            selector[2 + per_side * e + b, e * box_side + 1 + b] = 1.0
        selector[per_side * e + per_side + 3, e * box_side + box_side - 1] = 1.0
    box_z = jnp.asarray(selector @ np.kron(np.eye(elem_z), sine_np), jnp.float32)
    first_x = lax.axis_index("gx") == 0
    last_x = lax.axis_index("gx") == lax.axis_size("gx") - 1
    first_y = lax.axis_index("gy") == 0
    last_y = lax.axis_index("gy") == lax.axis_size("gy") - 1
    first_z = lax.axis_index("gz") == 0
    last_z = lax.axis_index("gz") == lax.axis_size("gz") - 1
    quad_x = jnp.asarray(np.tile(weights, elem_x), jnp.float32)
    quad_y = jnp.asarray(np.tile(weights, elem_y), jnp.float32)
    quad_z = jnp.asarray(np.tile(weights, elem_z), jnp.float32)
    weighted = coefficient * (quad_x[:, None, None] * quad_y[None, :, None] * quad_z[None, None, :])
    mask_in = jnp.where((jnp.arange(span_x) == span_x - 1) & last_x, 0.0, 1.0).astype(jnp.float32)[
        :, None, None
    ]
    multiplicity = (
        edge_weights(span_x, per_side, first_x, last_x)[:, None, None]
        * edge_weights(span_y, per_side, first_y, last_y)[None, :, None]
        * edge_weights(span_z, per_side, first_z, last_z)[None, None, :]
    )
    cell_mean = coefficient.reshape(elem_x, per_side, elem_y, per_side, elem_z, per_side).mean(
        axis=(1, 3, 5)
    )
    repeated = jnp.repeat(
        jnp.repeat(jnp.repeat(1.0 / cell_mean, box_side, 0), box_side, 1), box_side, 2
    )
    box_scale = repeated * jnp.asarray(np.tile(inverse, (elem_x, elem_y, elem_z)), jnp.float32)

    def precondition(wide_field):
        spectral = jnp.matmul(wide_field, box_z, precision=HIGHEST_MODE)
        for dim_id in (1, 0):
            spectral = along(partial(gather_boxes_first, per_side=per_side), spectral, dim_id)
            spectral = along(
                partial(contract_first, sine_basis, per_side=box_side), spectral, dim_id
            )
        spectral = spectral * box_scale
        for dim_id in (0, 1):
            spectral = along(
                partial(contract_first, sine_basis, per_side=box_side), spectral, dim_id
            )
            spectral = along(partial(scatter_boxes_first, per_side=per_side), spectral, dim_id)
        spread = jnp.matmul(spectral, box_z.T, precision=HIGHEST_MODE)
        widened = extended(spread, (("gx", 0), ("gy", 1), ("gz", 2)), 2)
        for dim_id in range(3):
            widened = along(fold_first, widened, dim_id)
        return mask_in * assemble_seams(widened, per_side)

    def margins_of(field):
        return extended(field, (("gx", 0), ("gy", 1), ("gz", 2)), 2)

    def inner_sum(first, second):
        return lax.psum(jnp.sum(multiplicity * first * second), ("gx", "gy", "gz"))

    solution = jnp.zeros_like(right_side)
    residual = mask_in * assemble_seams(right_side, per_side)
    precond = precondition(margins_of(residual))
    direction = precond
    rz_now = inner_sum(residual, precond)
    for iteration in range(ITERS):
        local_image = stiffness(direction, weighted, deriv_mat, kron_deriv)
        op_image = mask_in * assemble_seams(local_image, per_side)
        step_size = rz_now / inner_sum(direction, op_image)
        solution = solution + step_size * direction
        residual = residual - step_size * op_image
        if iteration + 1 < ITERS:
            precond = precondition(margins_of(residual))
            rz_next = inner_sum(residual, precond)
            direction = precond + rz_next / rz_now * direction
            rz_now = rz_next
    return (solution, residual)


def solution(mesh):
    placed = (P("gx", "gy", "gz"), P("gx", "gy", "gz"))
    return jax.shard_map(
        shards,
        mesh=mesh,
        in_specs=placed,
        out_specs=(P("gx", "gy", "gz"), P("gx", "gy", "gz")),
        check_vma=False,
    )
```

profile of v0, /device:TPU:1, one launch (start us, length us, event | category | flops | bytes accessed | tf_op | source)
XLA Modules:
  0.0 789.7 jit_solution(14626438956108496853)
XLA Ops:
  1.4 9.6 %collective-permute-start = (f32[1,32,128]{2,1,0:T(8,128)S(1)}, f32[1,32,128]{2,1,0:T(8,128)S(1)}, u32[]{:S(2)}, u32[]{:S(2)}) collective-permute-start(f32[1,32,128]{2,1,0:T(8,128)S(1)} %get-tuple-element.102), channel_id=1, source_target_pairs={{0,128},{128,256},{256,384},{1,129},{129,257},{257,385},{2,130},{1... | collective-permute-start | bytes 49160 | tf_op jit(solution)/shard_map/ppermute | solution.py:25
  13.3 7.6 collective-permute-done.1
  21.0 3.9 collective-permute-start.3
  24.9 3.1 collective-permute-start.2
  30.3 4.0 collective-permute-start.4
  34.5 6.6 collective-permute-done.5
  47.1 8.1 %collective-permute-start.6 = (f32[2,32,128]{2,1,0:T(8,128)S(1)}, f32[2,32,128]{2,1,0:T(8,128)S(1)}, u32[]{:S(2)}, u32[]{:S(2)}) collective-permute-start(f32[2,32,128]{2,1,0:T(8,128)S(1)} %get-tuple-element.99), channel_id=1, source_target_pairs={{0,128},{128,256},{256,384},{1,129},{129,257},{257,385},{2,130},{1... | collective-permute-start | bytes 98312 | tf_op jit(solution)/shard_map/ppermute | solution.py:25
  55.2 3.7 reshape.295
  61.5 2.7 collective-permute-start.9
  64.2 3.1 collective-permute-start.8
  70.6 5.5 collective-permute-start.10
  78.2 4.6 collective-permute-done.11
  105.9 8.1 %collective-permute-start.12 = (f32[2,36,132]{2,1,0:T(8,128)S(1)}, f32[2,36,132]{2,1,0:T(8,128)S(1)}, u32[]{:S(2)}, u32[]{:S(2)}) collective-permute-start(f32[2,36,132]{2,1,0:T(8,128)S(1)} %get-tuple-element.29), channel_id=1, source_target_pairs={{0,128},{128,256},{256,384},{1,129},{129,257},{257,385},{2,130},{1... | collective-permute-start | bytes 114056 | tf_op jit(solution)/shard_map/ppermute | solution.py:25
  115.8 3.4 collective-permute-start.15
  119.2 2.6 collective-permute-start.14
  124.7 5.6 collective-permute-start.16
  130.3 8.5 %collective-permute-done.17 = f32[24,40,2]{2,1,0:T(8,128)S(1)} collective-permute-done((f32[24,40,2]{2,1,0:T(8,128)S(1)}, f32[24,40,2]{2,1,0:T(8,128)S(1)}, u32[]{:S(2)}, u32[]{:S(2)}) %collective-permute-start.17) | collective-permute-done | bytes 7712 | tf_op jit(solution)/shard_map/ppermute | solution.py:27
  143.6 8.5 %collective-permute-start.18 = (f32[1,32,128]{2,1,0:T(8,128)S(1)}, f32[1,32,128]{2,1,0:T(8,128)S(1)}, u32[]{:S(2)}, u32[]{:S(2)}) collective-permute-start(f32[1,32,128]{2,1,0:T(8,128)S(1)} %get-tuple-element.97), channel_id=1, source_target_pairs={{0,128},{128,256},{256,384},{1,129},{129,257},{257,385},{2,130},{1... | collective-permute-start | bytes 49160 | tf_op jit(solution)/shard_map/ppermute | solution.py:25
  153.0 4.0 collective-permute-start.21
  162.3 5.9 collective-permute-start.22
  168.3 6.2 collective-permute-done.23
  185.0 17.0 %collective-permute-start.24 = (f32[1,32,128]{2,1,0:T(8,128)S(1)}, f32[1,32,128]{2,1,0:T(8,128)S(1)}, u32[]{:S(2)}, u32[]{:S(2)}) collective-permute-start(f32[1,32,128]{2,1,0:T(8,128)S(1)} %get-tuple-element.95), channel_id=1, source_target_pairs={{0,128},{128,256},{256,384},{1,129},{129,257},{257,385},{2,130},{1... | collective-permute-start | bytes 49160 | tf_op jit(solution)/shard_map/ppermute | solution.py:25
  202.9 2.9 collective-permute-start.27
  205.8 2.7 collective-permute-start.26
  210.7 4.8 collective-permute-start.28
  215.6 6.9 collective-permute-done.29
  228.8 142.4 %all-reduce.48 = (f32[]{:T(128)}, f32[]{:T(128)}) all-reduce(f32[]{:T(128)} %get-tuple-element.3, f32[]{:T(128)} %get-tuple-element.2), channel_id=1, replica_groups=mesh['gx'=4,'gy'=8,'gz'=16] {'gx','gy','gz'}, use_global_device_ids=true, to_apply=%region_2.3 | all-reduce | flops 2 | bytes 16 | tf_op jit(solution)/shard_map/psum | solution.py:238
  374.7 8.0 %collective-permute-start.30 = (f32[2,32,128]{2,1,0:T(8,128)S(1)}, f32[2,32,128]{2,1,0:T(8,128)S(1)}, u32[]{:S(2)}, u32[]{:S(2)}) collective-permute-start(f32[2,32,128]{2,1,0:T(8,128)S(1)} %get-tuple-element.93), channel_id=1, source_target_pairs={{0,128},{128,256},{256,384},{1,129},{129,257},{257,385},{2,130},{1... | collective-permute-start | bytes 98312 | tf_op jit(solution)/shard_map/ppermute | solution.py:25
  384.2 3.3 collective-permute-start.33
  392.2 4.0 collective-permute-start.34
  396.2 7.8 collective-permute-done.35
  407.3 2.7 convolution_bitcast_fusion.3
  413.5 2.6 slice.498
  428.0 8.4 %collective-permute-start.36 = (f32[2,36,132]{2,1,0:T(8,128)S(1)}, f32[2,36,132]{2,1,0:T(8,128)S(1)}, u32[]{:S(2)}, u32[]{:S(2)}) collective-permute-start(f32[2,36,132]{2,1,0:T(8,128)S(1)} %get-tuple-element.27), channel_id=1, source_target_pairs={{0,128},{128,256},{256,384},{1,129},{129,257},{257,385},{2,130},{1... | collective-permute-start | bytes 114056 | tf_op jit(solution)/shard_map/ppermute | solution.py:25
  438.0 12.6 %collective-permute-start.39 = (f32[24,2,132]{2,1,0:T(2,128)S(1)}, f32[24,2,132]{2,1,0:T(2,128)S(1)}, u32[]{:S(2)}, u32[]{:S(2)}) collective-permute-start(f32[24,2,132]{2,1,0:T(2,128)S(1)} %get-tuple-element.22), channel_id=1, source_target_pairs={{16,0},{32,16},{48,32},{64,48},{80,64},{96,80},{112,96},{17,1},{33... | collective-permute-start | bytes 76040 | tf_op jit(solution)/shard_map/ppermute | solution.py:27
  455.4 4.3 collective-permute-start.40
  459.7 19.5 %collective-permute-done.41 = f32[24,40,2]{2,1,0:T(8,128)S(1)} collective-permute-done((f32[24,40,2]{2,1,0:T(8,128)S(1)}, f32[24,40,2]{2,1,0:T(8,128)S(1)}, u32[]{:S(2)}, u32[]{:S(2)}) %collective-permute-start.41) | collective-permute-done | bytes 7712 | tf_op jit(solution)/shard_map/ppermute | solution.py:27
  482.2 7.9 collective-permute-start.42
  491.0 4.0 collective-permute-start.45
  495.0 2.8 collective-permute-start.44
  500.2 4.0 collective-permute-start.46
  504.2 15.0 %collective-permute-done.47 = f32[18,34,1]{2,1,0:T(8,128)S(1)} collective-permute-done((f32[18,34,1]{2,1,0:T(8,128)S(1)}, f32[18,34,1]{2,1,0:T(8,128)S(1)}, u32[]{:S(2)}, u32[]{:S(2)}) %collective-permute-start.47) | collective-permute-done | bytes 2480 | tf_op jit(solution)/shard_map/ppermute | solution.py:27
  523.4 116.0 %psum.30 = f32[]{:T(128)} all-reduce(f32[]{:T(128)} %get-tuple-element.8), channel_id=1, replica_groups=mesh['gx'=4,'gy'=8,'gz'=16] {'gx','gy','gz'}, use_global_device_ids=true, to_apply=%region_6.7 | all-reduce | flops 1 | bytes 8 | tf_op jit(solution)/shard_map/psum | solution.py:238
  644.9 7.9 collective-permute-start.48
  653.7 3.7 collective-permute-start.51
  662.3 4.0 collective-permute-start.52
  666.4 7.2 collective-permute-done.53
  676.9 109.5 %psum.31 = f32[]{:T(128)} all-reduce(f32[]{:T(128)} %get-tuple-element.6), channel_id=1, replica_groups=mesh['gx'=4,'gy'=8,'gz'=16] {'gx','gy','gz'}, use_global_device_ids=true, to_apply=%region_8.9 | all-reduce | flops 1 | bytes 8 | tf_op jit(solution)/shard_map/psum | solution.py:238
  (403 shorter events, 134.8 us)
Async XLA Ops:
  1.4 10.9 %collective-permute-start = (f32[1,32,128]{2,1,0:T(8,128)S(1)}, f32[1,32,128]{2,1,0:T(8,128)S(1)}, u32[]{:S(2)}, u32[]{:S(2)}) collective-permute-start(f32[1,32,128]{2,1,0:T(8,128)S(1)} %get-tuple-element.102), channel_id=1, source_target_pairs={{0,128},{128,256},{256,384},{1,129},{129,257},{257,385},{2,130},{1... | collective-permute-start | bytes 49160 | tf_op jit(solution)/shard_map/ppermute | solution.py:25
  11.0 9.9 %collective-permute-start.1 = (f32[1,32,128]{2,1,0:T(8,128)S(1)}, f32[1,32,128]{2,1,0:T(8,128)S(1)}, u32[]{:S(2)}, u32[]{:S(2)}) collective-permute-start(f32[1,32,128]{2,1,0:T(8,128)S(1)} %get-tuple-element.101), channel_id=1, source_target_pairs={{128,0},{256,128},{384,256},{129,1},{257,129},{385,257},{130,2},{2... | collective-permute-start | bytes 49160 | tf_op jit(solution)/shard_map/ppermute | solution.py:27
  21.0 7.0 collective-permute-start.3
  24.9 3.9 collective-permute-start.2
  29.0 12.1 %collective-permute-start.5 = (f32[18,34,1]{2,1,0:T(8,128)S(1)}, f32[18,34,1]{2,1,0:T(8,128)S(1)}, u32[]{:S(2)}, u32[]{:S(2)}) collective-permute-start(f32[18,34,1]{2,1,0:T(8,128)S(1)} %get-tuple-element.74), channel_id=1, source_target_pairs={{1,0},{2,1},{3,2},{4,3},{5,4},{6,5},{7,6},{8,7},{9,8},{10,9},{11,1... | collective-permute-start | bytes 7352 | tf_op jit(solution)/shard_map/ppermute | solution.py:27
  30.3 12.3 %collective-permute-start.4 = (f32[18,34,1]{2,1,0:T(8,128)S(1)}, f32[18,34,1]{2,1,0:T(8,128)S(1)}, u32[]{:S(2)}, u32[]{:S(2)}) collective-permute-start(f32[18,34,1]{2,1,0:T(8,128)S(1)} %get-tuple-element.73), channel_id=1, source_target_pairs={{0,1},{1,2},{2,3},{3,4},{4,5},{5,6},{6,7},{7,8},{8,9},{9,10},{10,1... | collective-permute-start | bytes 7352 | tf_op jit(solution)/shard_map/ppermute | solution.py:25
  45.8 15.7 %collective-permute-start.7 = (f32[2,32,128]{2,1,0:T(8,128)S(1)}, f32[2,32,128]{2,1,0:T(8,128)S(1)}, u32[]{:S(2)}, u32[]{:S(2)}) collective-permute-start(f32[2,32,128]{2,1,0:T(8,128)S(1)} %get-tuple-element.100), channel_id=1, source_target_pairs={{128,0},{256,128},{384,256},{129,1},{257,129},{385,257},{130,2},{2... | collective-permute-start | bytes 98312 | tf_op jit(solution)/shard_map/ppermute | solution.py:27
  47.1 14.4 %collective-permute-start.6 = (f32[2,32,128]{2,1,0:T(8,128)S(1)}, f32[2,32,128]{2,1,0:T(8,128)S(1)}, u32[]{:S(2)}, u32[]{:S(2)}) collective-permute-start(f32[2,32,128]{2,1,0:T(8,128)S(1)} %get-tuple-element.99), channel_id=1, source_target_pairs={{0,128},{128,256},{256,384},{1,129},{129,257},{257,385},{2,130},{1... | collective-permute-start | bytes 98312 | tf_op jit(solution)/shard_map/ppermute | solution.py:25
  61.5 6.2 collective-permute-start.9
  64.2 4.0 collective-permute-start.8
  69.3 13.6 %collective-permute-start.11 = (f32[20,36,2]{2,1,0:T(8,128)}, f32[20,36,2]{2,1,0:T(8,128)}, u32[]{:S(2)}, u32[]{:S(2)}) collective-permute-start(f32[20,36,2]{2,1,0:T(8,128)} %get-tuple-element.64), channel_id=1, source_target_pairs={{1,0},{2,1},{3,2},{4,3},{5,4},{6,5},{7,6},{8,7},{9,8},{10,9},{11,1... | collective-permute-start | bytes 17288 | tf_op jit(solution)/shard_map/ppermute | solution.py:27
  70.6 14.0 %collective-permute-start.10 = (f32[20,36,2]{2,1,0:T(8,128)}, f32[20,36,2]{2,1,0:T(8,128)}, u32[]{:S(2)}, u32[]{:S(2)}) collective-permute-start(f32[20,36,2]{2,1,0:T(8,128)} %get-tuple-element.63), channel_id=1, source_target_pairs={{0,1},{1,2},{2,3},{3,4},{4,5},{5,6},{6,7},{7,8},{8,9},{9,10},{10,1... | collective-permute-start | bytes 17288 | tf_op jit(solution)/shard_map/ppermute | solution.py:25
  104.6 10.2 %collective-permute-start.13 = (f32[2,36,132]{2,1,0:T(8,128)S(1)}, f32[2,36,132]{2,1,0:T(8,128)S(1)}, u32[]{:S(2)}, u32[]{:S(2)}) collective-permute-start(f32[2,36,132]{2,1,0:T(8,128)S(1)} %get-tuple-element.30), channel_id=1, source_target_pairs={{128,0},{256,128},{384,256},{129,1},{257,129},{385,257},{130,2},{2... | collective-permute-start | bytes 114056 | tf_op jit(solution)/shard_map/ppermute | solution.py:27
  105.9 9.8 %collective-permute-start.12 = (f32[2,36,132]{2,1,0:T(8,128)S(1)}, f32[2,36,132]{2,1,0:T(8,128)S(1)}, u32[]{:S(2)}, u32[]{:S(2)}) collective-permute-start(f32[2,36,132]{2,1,0:T(8,128)S(1)} %get-tuple-element.29), channel_id=1, source_target_pairs={{0,128},{128,256},{256,384},{1,129},{129,257},{257,385},{2,130},{1... | collective-permute-start | bytes 114056 | tf_op jit(solution)/shard_map/ppermute | solution.py:25
  115.8 6.1 collective-permute-start.15
  119.2 3.8 collective-permute-start.14
  123.4 15.4 %collective-permute-start.17 = (f32[24,40,2]{2,1,0:T(8,128)S(1)}, f32[24,40,2]{2,1,0:T(8,128)S(1)}, u32[]{:S(2)}, u32[]{:S(2)}) collective-permute-start(f32[24,40,2]{2,1,0:T(8,128)S(1)} %get-tuple-element.24), channel_id=1, source_target_pairs={{1,0},{2,1},{3,2},{4,3},{5,4},{6,5},{7,6},{8,7},{9,8},{10,9},{11,1... | collective-permute-start | bytes 23048 | tf_op jit(solution)/shard_map/ppermute | solution.py:27
  124.7 15.9 %collective-permute-start.16 = (f32[24,40,2]{2,1,0:T(8,128)S(1)}, f32[24,40,2]{2,1,0:T(8,128)S(1)}, u32[]{:S(2)}, u32[]{:S(2)}) collective-permute-start(f32[24,40,2]{2,1,0:T(8,128)S(1)} %get-tuple-element.23), channel_id=1, source_target_pairs={{0,1},{1,2},{2,3},{3,4},{4,5},{5,6},{6,7},{7,8},{8,9},{9,10},{10,1... | collective-permute-start | bytes 23048 | tf_op jit(solution)/shard_map/ppermute | solution.py:25
  142.3 9.8 %collective-permute-start.19 = (f32[1,32,128]{2,1,0:T(8,128)S(1)}, f32[1,32,128]{2,1,0:T(8,128)S(1)}, u32[]{:S(2)}, u32[]{:S(2)}) collective-permute-start(f32[1,32,128]{2,1,0:T(8,128)S(1)} %get-tuple-element.98), channel_id=1, source_target_pairs={{128,0},{256,128},{384,256},{129,1},{257,129},{385,257},{130,2},{2... | collective-permute-start | bytes 49160 | tf_op jit(solution)/shard_map/ppermute | solution.py:27
  143.6 9.3 %collective-permute-start.18 = (f32[1,32,128]{2,1,0:T(8,128)S(1)}, f32[1,32,128]{2,1,0:T(8,128)S(1)}, u32[]{:S(2)}, u32[]{:S(2)}) collective-permute-start(f32[1,32,128]{2,1,0:T(8,128)S(1)} %get-tuple-element.97), channel_id=1, source_target_pairs={{0,128},{128,256},{256,384},{1,129},{129,257},{257,385},{2,130},{1... | collective-permute-start | bytes 49160 | tf_op jit(solution)/shard_map/ppermute | solution.py:25
  153.0 6.1 collective-permute-start.21
  161.0 13.5 %collective-permute-start.23 = (f32[18,34,1]{2,1,0:T(8,128)}, f32[18,34,1]{2,1,0:T(8,128)S(1)}, u32[]{:S(2)}, u32[]{:S(2)}) collective-permute-start(f32[18,34,1]{2,1,0:T(8,128)} %get-tuple-element.72), channel_id=1, source_target_pairs={{1,0},{2,1},{3,2},{4,3},{5,4},{6,5},{7,6},{8,7},{9,8},{10,9},{11,1... | collective-permute-start | bytes 7352 | tf_op jit(solution)/shard_map/ppermute | solution.py:27
  162.3 13.8 %collective-permute-start.22 = (f32[18,34,1]{2,1,0:T(8,128)S(1)}, f32[18,34,1]{2,1,0:T(8,128)S(1)}, u32[]{:S(2)}, u32[]{:S(2)}) collective-permute-start(f32[18,34,1]{2,1,0:T(8,128)S(1)} %get-tuple-element.71), channel_id=1, source_target_pairs={{0,1},{1,2},{2,3},{3,4},{4,5},{5,6},{6,7},{7,8},{8,9},{9,10},{10,1... | collective-permute-start | bytes 7352 | tf_op jit(solution)/shard_map/ppermute | solution.py:25
  183.7 18.3 %collective-permute-start.25 = (f32[1,32,128]{2,1,0:T(8,128)S(1)}, f32[1,32,128]{2,1,0:T(8,128)S(1)}, u32[]{:S(2)}, u32[]{:S(2)}) collective-permute-start(f32[1,32,128]{2,1,0:T(8,128)S(1)} %get-tuple-element.96), channel_id=1, source_target_pairs={{128,0},{256,128},{384,256},{129,1},{257,129},{385,257},{130,2},{2... | collective-permute-start | bytes 49160 | tf_op jit(solution)/shard_map/ppermute | solution.py:27
  185.0 17.8 %collective-permute-start.24 = (f32[1,32,128]{2,1,0:T(8,128)S(1)}, f32[1,32,128]{2,1,0:T(8,128)S(1)}, u32[]{:S(2)}, u32[]{:S(2)}) collective-permute-start(f32[1,32,128]{2,1,0:T(8,128)S(1)} %get-tuple-element.95), channel_id=1, source_target_pairs={{0,128},{128,256},{256,384},{1,129},{129,257},{257,385},{2,130},{1... | collective-permute-start | bytes 49160 | tf_op jit(solution)/shard_map/ppermute | solution.py:25
  202.9 5.7 collective-permute-start.27
  209.4 13.1 %collective-permute-start.29 = (f32[18,34,1]{2,1,0:T(8,128)S(1)}, f32[18,34,1]{2,1,0:T(8,128)S(1)}, u32[]{:S(2)}, u32[]{:S(2)}) collective-permute-start(f32[18,34,1]{2,1,0:T(8,128)S(1)} %get-tuple-element.70), channel_id=1, source_target_pairs={{1,0},{2,1},{3,2},{4,3},{5,4},{6,5},{7,6},{8,7},{9,8},{10,9},{11,1... | collective-permute-start | bytes 7352 | tf_op jit(solution)/shard_map/ppermute | solution.py:27
  210.7 13.0 %collective-permute-start.28 = (f32[18,34,1]{2,1,0:T(8,128)S(1)}, f32[18,34,1]{2,1,0:T(8,128)S(1)}, u32[]{:S(2)}, u32[]{:S(2)}) collective-permute-start(f32[18,34,1]{2,1,0:T(8,128)S(1)} %get-tuple-element.69), channel_id=1, source_target_pairs={{0,1},{1,2},{2,3},{3,4},{4,5},{5,6},{6,7},{7,8},{8,9},{9,10},{10,1... | collective-permute-start | bytes 7352 | tf_op jit(solution)/shard_map/ppermute | solution.py:25
  373.4 10.7 %collective-permute-start.31 = (f32[2,32,128]{2,1,0:T(8,128)S(1)}, f32[2,32,128]{2,1,0:T(8,128)S(1)}, u32[]{:S(2)}, u32[]{:S(2)}) collective-permute-start(f32[2,32,128]{2,1,0:T(8,128)S(1)} %get-tuple-element.94), channel_id=1, source_target_pairs={{128,0},{256,128},{384,256},{129,1},{257,129},{385,257},{130,2},{2... | collective-permute-start | bytes 98312 | tf_op jit(solution)/shard_map/ppermute | solution.py:27
  374.7 9.4 %collective-permute-start.30 = (f32[2,32,128]{2,1,0:T(8,128)S(1)}, f32[2,32,128]{2,1,0:T(8,128)S(1)}, u32[]{:S(2)}, u32[]{:S(2)}) collective-permute-start(f32[2,32,128]{2,1,0:T(8,128)S(1)} %get-tuple-element.93), channel_id=1, source_target_pairs={{0,128},{128,256},{256,384},{1,129},{129,257},{257,385},{2,130},{1... | collective-permute-start | bytes 98312 | tf_op jit(solution)/shard_map/ppermute | solution.py:25
  384.2 5.6 collective-permute-start.33
  390.9 13.1 %collective-permute-start.35 = (f32[20,36,2]{2,1,0:T(8,128)S(1)}, f32[20,36,2]{2,1,0:T(8,128)S(1)}, u32[]{:S(2)}, u32[]{:S(2)}) collective-permute-start(f32[20,36,2]{2,1,0:T(8,128)S(1)} %get-tuple-element.62), channel_id=1, source_target_pairs={{1,0},{2,1},{3,2},{4,3},{5,4},{6,5},{7,6},{8,7},{9,8},{10,9},{11,1... | collective-permute-start | bytes 17288 | tf_op jit(solution)/shard_map/ppermute | solution.py:27
  392.2 12.4 %collective-permute-start.34 = (f32[20,36,2]{2,1,0:T(8,128)S(1)}, f32[20,36,2]{2,1,0:T(8,128)S(1)}, u32[]{:S(2)}, u32[]{:S(2)}) collective-permute-start(f32[20,36,2]{2,1,0:T(8,128)S(1)} %get-tuple-element.61), channel_id=1, source_target_pairs={{0,1},{1,2},{2,3},{3,4},{4,5},{5,6},{6,7},{7,8},{8,9},{9,10},{10,1... | collective-permute-start | bytes 17288 | tf_op jit(solution)/shard_map/ppermute | solution.py:25
  426.7 9.7 %collective-permute-start.37 = (f32[2,36,132]{2,1,0:T(8,128)S(1)}, f32[2,36,132]{2,1,0:T(8,128)S(1)}, u32[]{:S(2)}, u32[]{:S(2)}) collective-permute-start(f32[2,36,132]{2,1,0:T(8,128)S(1)} %get-tuple-element.28), channel_id=1, source_target_pairs={{128,0},{256,128},{384,256},{129,1},{257,129},{385,257},{130,2},{2... | collective-permute-start | bytes 114056 | tf_op jit(solution)/shard_map/ppermute | solution.py:27
  428.0 9.9 %collective-permute-start.36 = (f32[2,36,132]{2,1,0:T(8,128)S(1)}, f32[2,36,132]{2,1,0:T(8,128)S(1)}, u32[]{:S(2)}, u32[]{:S(2)}) collective-permute-start(f32[2,36,132]{2,1,0:T(8,128)S(1)} %get-tuple-element.27), channel_id=1, source_target_pairs={{0,128},{128,256},{256,384},{1,129},{129,257},{257,385},{2,130},{1... | collective-permute-start | bytes 114056 | tf_op jit(solution)/shard_map/ppermute | solution.py:25
  438.0 14.6 %collective-permute-start.39 = (f32[24,2,132]{2,1,0:T(2,128)S(1)}, f32[24,2,132]{2,1,0:T(2,128)S(1)}, u32[]{:S(2)}, u32[]{:S(2)}) collective-permute-start(f32[24,2,132]{2,1,0:T(2,128)S(1)} %get-tuple-element.22), channel_id=1, source_target_pairs={{16,0},{32,16},{48,32},{64,48},{80,64},{96,80},{112,96},{17,1},{33... | collective-permute-start | bytes 76040 | tf_op jit(solution)/shard_map/ppermute | solution.py:27
  454.1 25.1 %collective-permute-start.41 = (f32[24,40,2]{2,1,0:T(8,128)S(1)}, f32[24,40,2]{2,1,0:T(8,128)S(1)}, u32[]{:S(2)}, u32[]{:S(2)}) collective-permute-start(f32[24,40,2]{2,1,0:T(8,128)S(1)} %get-tuple-element.20), channel_id=1, source_target_pairs={{1,0},{2,1},{3,2},{4,3},{5,4},{6,5},{7,6},{8,7},{9,8},{10,9},{11,1... | collective-permute-start | bytes 23048 | tf_op jit(solution)/shard_map/ppermute | solution.py:27
  455.4 23.8 %collective-permute-start.40 = (f32[24,40,2]{2,1,0:T(8,128)S(1)}, f32[24,40,2]{2,1,0:T(8,128)S(1)}, u32[]{:S(2)}, u32[]{:S(2)}) collective-permute-start(f32[24,40,2]{2,1,0:T(8,128)S(1)} %get-tuple-element.19), channel_id=1, source_target_pairs={{0,1},{1,2},{2,3},{3,4},{4,5},{5,6},{6,7},{7,8},{8,9},{9,10},{10,1... | collective-permute-start | bytes 23048 | tf_op jit(solution)/shard_map/ppermute | solution.py:25
  480.9 9.2 %collective-permute-start.43 = (f32[1,32,128]{2,1,0:T(8,128)S(1)}, f32[1,32,128]{2,1,0:T(8,128)S(1)}, u32[]{:S(2)}, u32[]{:S(2)}) collective-permute-start(f32[1,32,128]{2,1,0:T(8,128)S(1)} %get-tuple-element.92), channel_id=1, source_target_pairs={{128,0},{256,128},{384,256},{129,1},{257,129},{385,257},{130,2},{2... | collective-permute-start | bytes 49160 | tf_op jit(solution)/shard_map/ppermute | solution.py:27
  482.2 8.8 %collective-permute-start.42 = (f32[1,32,128]{2,1,0:T(8,128)S(1)}, f32[1,32,128]{2,1,0:T(8,128)S(1)}, u32[]{:S(2)}, u32[]{:S(2)}) collective-permute-start(f32[1,32,128]{2,1,0:T(8,128)S(1)} %get-tuple-element.91), channel_id=1, source_target_pairs={{0,128},{128,256},{256,384},{1,129},{129,257},{257,385},{2,130},{1... | collective-permute-start | bytes 49160 | tf_op jit(solution)/shard_map/ppermute | solution.py:25
  491.0 6.8 collective-permute-start.45
  498.9 20.3 %collective-permute-start.47 = (f32[18,34,1]{2,1,0:T(8,128)S(1)}, f32[18,34,1]{2,1,0:T(8,128)S(1)}, u32[]{:S(2)}, u32[]{:S(2)}) collective-permute-start(f32[18,34,1]{2,1,0:T(8,128)S(1)} %get-tuple-element.68), channel_id=1, source_target_pairs={{1,0},{2,1},{3,2},{4,3},{5,4},{6,5},{7,6},{8,7},{9,8},{10,9},{11,1... | collective-permute-start | bytes 7352 | tf_op jit(solution)/shard_map/ppermute | solution.py:27
  500.2 19.0 %collective-permute-start.46 = (f32[18,34,1]{2,1,0:T(8,128)S(1)}, f32[18,34,1]{2,1,0:T(8,128)S(1)}, u32[]{:S(2)}, u32[]{:S(2)}) collective-permute-start(f32[18,34,1]{2,1,0:T(8,128)S(1)} %get-tuple-element.67), channel_id=1, source_target_pairs={{0,1},{1,2},{2,3},{3,4},{4,5},{5,6},{6,7},{7,8},{8,9},{9,10},{10,1... | collective-permute-start | bytes 7352 | tf_op jit(solution)/shard_map/ppermute | solution.py:25
  643.6 9.2 %collective-permute-start.49 = (f32[1,32,128]{2,1,0:T(8,128)S(1)}, f32[1,32,128]{2,1,0:T(8,128)S(1)}, u32[]{:S(2)}, u32[]{:S(2)}) collective-permute-start(f32[1,32,128]{2,1,0:T(8,128)S(1)} %get-tuple-element.90), channel_id=1, source_target_pairs={{128,0},{256,128},{384,256},{129,1},{257,129},{385,257},{130,2},{2... | collective-permute-start | bytes 49160 | tf_op jit(solution)/shard_map/ppermute | solution.py:27
  644.9 8.8 %collective-permute-start.48 = (f32[1,32,128]{2,1,0:T(8,128)S(1)}, f32[1,32,128]{2,1,0:T(8,128)S(1)}, u32[]{:S(2)}, u32[]{:S(2)}) collective-permute-start(f32[1,32,128]{2,1,0:T(8,128)S(1)} %get-tuple-element.89), channel_id=1, source_target_pairs={{0,128},{128,256},{256,384},{1,129},{129,257},{257,385},{2,130},{1... | collective-permute-start | bytes 49160 | tf_op jit(solution)/shard_map/ppermute | solution.py:25
  653.7 6.4 collective-permute-start.51
  661.1 12.5 %collective-permute-start.53 = (f32[18,34,1]{2,1,0:T(8,128)S(1)}, f32[18,34,1]{2,1,0:T(8,128)S(1)}, u32[]{:S(2)}, u32[]{:S(2)}) collective-permute-start(f32[18,34,1]{2,1,0:T(8,128)S(1)} %get-tuple-element.66), channel_id=1, source_target_pairs={{1,0},{2,1},{3,2},{4,3},{5,4},{6,5},{7,6},{8,7},{9,8},{10,9},{11,1... | collective-permute-start | bytes 7352 | tf_op jit(solution)/shard_map/ppermute | solution.py:27
  662.3 11.9 %collective-permute-start.52 = (f32[18,34,1]{2,1,0:T(8,128)S(1)}, f32[18,34,1]{2,1,0:T(8,128)S(1)}, u32[]{:S(2)}, u32[]{:S(2)}) collective-permute-start(f32[18,34,1]{2,1,0:T(8,128)S(1)} %get-tuple-element.65), channel_id=1, source_target_pairs={{0,1},{1,2},{2,3},{3,4},{4,5},{5,6},{6,7},{7,8},{8,9},{9,10},{10,1... | collective-permute-start | bytes 7352 | tf_op jit(solution)/shard_map/ppermute | solution.py:25
  (80 other events, 608.2 us)
where the time goes:
time: 797 us; the launch traced here: 790 us
  blocking collectives  368 us (46%)
  starting transfers between devices  213 us (27%)
  waiting for transfers between devices  115 us (14%)
  local copies, waits for them, and re-layouts  43 us (5%)
  matrix products  23.5 us (3%)
  other arithmetic  20.7 us (3%)
    psum x3, blocking collectives, inner_sum(): return lax.psum(jnp.sum(multiplicity * first * second), ('gx', 'gy', 'gz'))  368 us
    ppermute x27, starting transfers between devices, extended(): lax.ppermute(tail, axis, [(i, (i + 1) % count) for i in range(ends)])  149 us
    ppermute x27, waiting for transfers between devices, extended(): lax.ppermute(head, axis, [((i + 1) % count, i) for i in range(ends)])  92.1 us
    ppermute x27, starting transfers between devices, extended(): lax.ppermute(head, axis, [((i + 1) % count, i) for i in range(ends)])  64 us
    ppermute x27, waiting for transfers between devices, extended(): lax.ppermute(tail, axis, [(i, (i + 1) % count) for i in range(ends)])  22.6 us
    dot_general x16, matrix products, contract_first(): jnp.einsum('ij,aj...->ai...', matrix, shaped, precision=HIGHEST_MODE)  17.1 us
  transfers between devices with their start and end apart: 54, of which 34 were waited for; matrix products, arithmetic and copies ran while one was open for 1% of the time, Pallas kernels for 0%

commit v1 on v0

v1 whole, which is shorter than its diff:
```python
import itertools

import jax
import jax.numpy as jnp
import numpy as np
from jax import lax
from jax.experimental import pallas as pl
from jax.experimental.pallas import tpu as pltpu
from jax.sharding import PartitionSpec as P

ORDER = 7
SIDE = ORDER + 1
BOX = ORDER + 3
AXES = ("gx", "gy", "gz")
MESH = pl.DeviceIdType.MESH
F32 = jnp.float32
NEAR = [o for o in itertools.product((-1, 0, 1), repeat=3) if o != (0, 0, 0)]


def legendre_rows(points, degree):
    table_rows = [np.ones(points.shape), points * 1.0]
    for k in range(2, degree + 1):
        table_rows.append(
            ((2 * k - 1) * points * table_rows[k - 1] - (k - 1) * table_rows[k - 2]) / k
        )
    return table_rows


def lobatto_tables(degree):
    per_side = degree + 1
    points = np.cos(np.pi * np.arange(per_side) / degree)
    for newton_step in range(60):
        table_rows = legendre_rows(points, degree)
        points = points - (points * table_rows[degree] - table_rows[degree - 1]) / (
            per_side * table_rows[degree]
        )
    top_row = legendre_rows(points, degree)[degree][::-1]
    points = points[::-1]
    weights = 2.0 / (degree * per_side * top_row**2)
    deriv_np = np.zeros((per_side, per_side))
    for a in range(per_side):
        for b in range(per_side):
            if a != b:
                deriv_np[a, b] = top_row[a] / (top_row[b] * (points[a] - points[b]))
    deriv_np[0, 0] = -degree * per_side / 4.0
    deriv_np[-1, -1] = degree * per_side / 4.0
    return (weights, deriv_np)


def sine_tables(degree):
    box_side = degree + 3
    grid_index = np.arange(1, box_side + 1)
    sine_np = np.sqrt(2.0 / (box_side + 1)) * np.sin(
        np.pi * np.outer(grid_index, grid_index) / (box_side + 1)
    )
    eigen_values = 2.0 - 2.0 * np.cos(np.pi * grid_index / (box_side + 1))
    summed = eigen_values[:, None, None] + eigen_values[None, :, None] + eigen_values[None, None, :]
    return (sine_np, 1.0 / summed)


WEIGHTS, DERIV = lobatto_tables(ORDER)
SINE, INVERSE = sine_tables(ORDER)


def z_tables(elements):
    span = elements * SIDE
    assemble = np.zeros((span + 2, 2 * span))
    for i in range(span):
        assemble[1 + i, i] = 1.0
        if i % SIDE == 0 and i > 0:
            assemble[1 + i, i - 1] = 1.0
        if i % SIDE == SIDE - 1 and i < span - 1:
            assemble[1 + i, i + 1] = 1.0
    assemble[0, span] = 1.0
    assemble[1, span + 1] = 1.0
    assemble[span, 2 * span - 2] = 1.0
    assemble[span + 1, 2 * span - 1] = 1.0
    gather = np.zeros((elements * BOX, span + 2))
    for e in range(elements):
        gather[e * BOX, 0 if e == 0 else 1 + SIDE * e - 2] = 1.0
        for k in range(SIDE):
            gather[e * BOX + 1 + k, 1 + SIDE * e + k] = 1.0
        gather[e * BOX + BOX - 1, span + 1 if e == elements - 1 else 1 + SIDE * (e + 1) + 1] = 1.0
    to_modes = np.kron(np.eye(elements), SINE) @ gather @ assemble
    forward = np.zeros((2 * span, 2 * span))
    forward[:, : elements * BOX] = to_modes.T
    return forward, assemble[1:-1].T


def rotate(x, shift, axis):
    return pltpu.roll(x, shift % x.shape[axis], axis)


class Halo:
    def __init__(self, n, hf, hs, lf, ls):
        self.n, self.hf, self.hs, self.lf, self.ls = n, hf, hs, lf, ls
        self.packed = 4 * n + 4
        self.own_z = -(-n * n // 64)
        self.z_hi = self.packed
        self.z_lo = self.packed + self.own_z + 1
        self.total = self.packed + 2 * (self.own_z + 1)
        self.slot, at = {}, 0
        for o in NEAR:
            self.slot[o] = (at, self.part(o)[1])
            at += self.part(o)[1]
        self.received = at

    def part(self, o):
        n = self.n
        if o[2]:
            base = self.z_hi if o[2] > 0 else self.z_lo
            return (base, self.own_z) if o[:2] == (0, 0) else (base + self.own_z, 1)
        if o[0] == 0:
            return (0 if o[1] > 0 else n, n)
        if o[1] == 0:
            return (2 * n if o[0] > 0 else 3 * n, n)
        return (4 * n + {(1, 1): 0, (1, -1): 1, (-1, 1): 2, (-1, -1): 3}[o[:2]], 1)


IN = Halo(SIDE, 7, 6, 0, 1)
OUT = Halo(BOX, 8, 9, 1, 0)
RED = (8, 4, 16)


def make_kernel(sizes, z_run):
    nx, ny, nz = sizes
    runs = nz // z_run
    ring = nx * z_run

    def kernel(b_ref, c_ref, wyz_ref, fwd_ref, bwd_ref, asm_ref, der_ref, inv_ref, mean_ref,
               sol_ref, res_ref,
               rows, raw, wc, icb, gs, gr, ug, e, x, sp, c1p, ss, sr, us, zs, acc,
               red_y, red_x, red_z, gsend, grecv, ssend, srecv, rsend, rrecv):
        gx, gy, gz = (lax.axis_index(a) for a in AXES)

        def near(o):
            return ((gx + o[0] + nx) % nx, (gy + o[1] + ny) % ny, (gz + o[2] + nz) % nz)

        def ring_y(t):
            return (gx, (gy + t) % ny, gz)

        def ring_x(t):
            return (gx, gy, ((gz // z_run + t) % runs) * z_run + gz % z_run)

        def ring_z(t):
            to = (gx * z_run + gz % z_run + t) % ring
            return (to // z_run, gy, (gz // z_run) * z_run + to % z_run)

        partners = [near(o) for o in NEAR]
        partners += [ring_y(t) for t in range(1, ny)]
        partners += [ring_x(t) for t in range(1, runs)]
        partners += [ring_z(t) for t in range(1, ring)]
        barrier = pltpu.get_barrier_semaphore()
        for device in partners:
            pl.semaphore_signal(barrier, inc=1, device_id=device, device_id_type=MESH)

        sub = lax.broadcasted_iota(jnp.int32, (8, 128), 0)
        lane = lax.broadcasted_iota(jnp.int32, (8, 128), 1)
        pair = lane // 2
        ey = sub % 4
        lower = sub < 4

        def flag(condition):
            return jnp.where(condition, 1.0, 0.0).astype(F32)

        fx_lo, fx_hi = flag(gx > 0), flag(gx < nx - 1)
        fy_lo, fy_hi = flag(gy > 0), flag(gy < ny - 1)
        fz_lo, fz_hi = flag(gz > 0), flag(gz < nz - 1)
        y_mask = jnp.where(ey >= 2, fy_lo, fy_hi)
        z_mask = jnp.where(lane < 2, fz_lo, jnp.where(lane >= 126, fz_hi, 0.0))
        x_mask = jnp.where(lower, 1.0, fx_hi)

        def pack(u, halo):
            y_hi = jnp.where(ey == 3, u[:, halo.hf], rotate(u[:, halo.hs], 7, 1))
            y_lo = jnp.where(ey == 0, u[:, halo.lf], rotate(u[:, halo.ls], 1, 1))
            x_hi = jnp.where(lower, rotate(u[halo.hs], 4, 1), u[halo.hf])
            x_lo = jnp.where(lower, u[halo.lf], rotate(u[halo.ls], 4, 1))
            corner = [
                jnp.where(lower, rotate(y_hi[halo.hs], 4, 0), y_hi[halo.hf]),
                jnp.where(lower, rotate(y_lo[halo.hs], 4, 0), y_lo[halo.hf]),
                jnp.where(lower, y_hi[halo.lf], rotate(y_hi[halo.ls], 4, 0)),
                jnp.where(lower, y_lo[halo.lf], rotate(y_lo[halo.ls], 4, 0)),
            ]
            return y_hi, y_lo, x_hi, x_lo, corner

        def store_packed(ref, parts, n):
            for k in range(4):
                ref[k * n : (k + 1) * n] = parts[k]
            for k in range(4):
                ref[4 * n + k] = parts[4][k]

        def lane_pack(values, up):
            total = None
            for k, value in enumerate(values):
                moved = rotate(value, 2 * k + 2 if up else 2 * k, 1)
                total = moved if total is None else jnp.where(pair == k, moved, total)
            return total

        def send(src, dst, halo, send_sem, recv_sem):
            for o in NEAR:
                at, count = halo.part(o)
                to, _ = halo.slot[(-o[0], -o[1], -o[2])]
                pltpu.make_async_remote_copy(
                    src_ref=src.at[pl.ds(at, count)],
                    dst_ref=dst.at[pl.ds(to, count)],
                    send_sem=send_sem,
                    recv_sem=recv_sem,
                    device_id=near(o),
                    device_id_type=MESH,
                ).start()

        def wait_all(ref, sem):
            pltpu.make_async_copy(ref, ref, sem).wait()

        def merged_lanes(dst, halo, dz):
            n = halo.n

            def got(dx, dy):
                return dst[halo.slot[(dx, dy, dz)][0]]

            out = jnp.where(ey >= 2, got(0, -1), rotate(got(0, 1), -2 * n, 1))
            out = jnp.where(pair >= 2 * n, got(-1, 0), out)
            out = jnp.where(pair >= 3 * n, got(1, 0), out)
            low = jnp.where(ey >= 2, got(-1, -1), rotate(got(-1, 1), -2, 1))
            high = jnp.where(ey >= 2, got(1, -1), rotate(got(1, 1), -2, 1))
            out = jnp.where(pair >= 4 * n, low, out)
            return jnp.where(pair >= 4 * n + 2, high, out)

        def unlane(low, high, k):
            return z_mask * jnp.where(
                lane < 2, rotate(low, -2 * k, 1), rotate(high, 126 - 2 * k, 1)
            )

        def receive(dst, halo, put):
            n = halo.n

            def at(o, k=0):
                return dst[halo.slot[o][0] + k]

            own_lo = [dst[halo.slot[(0, 0, -1)][0] + k] for k in range(halo.own_z)]
            own_hi = [dst[halo.slot[(0, 0, 1)][0] + k] for k in range(halo.own_z)]
            for i in range(n):
                for j in range(n):
                    k = i * n + j
                    put(1, i, j, unlane(own_lo[k // 64], own_hi[k // 64], k % 64))
            low, high = merged_lanes(dst, halo, -1), merged_lanes(dst, halo, 1)
            for k in range(n):
                put(0, k, n, y_mask * jnp.where(ey >= 2, at((0, -1, 0), k), at((0, 1, 0), k)))
                put(1, k, n, y_mask * unlane(low, high, k))
                put(0, n, k, fx_lo * at((-1, 0, 0), k))
                put(1, n, k, fx_lo * unlane(low, high, 2 * n + k))
                put(0, n + 1, k, fx_hi * at((1, 0, 0), k))
                put(1, n + 1, k, fx_hi * unlane(low, high, 3 * n + k))
            put(0, n, n, fx_lo * y_mask * jnp.where(ey >= 2, at((-1, -1, 0)), at((-1, 1, 0))))
            put(1, n, n, fx_lo * y_mask * unlane(low, high, 4 * n))
            put(0, n + 1, n, fx_hi * y_mask * jnp.where(ey >= 2, at((1, -1, 0)), at((1, 1, 0))))
            put(1, n + 1, n, fx_hi * y_mask * unlane(low, high, 4 * n + 2))

        def from_x(u, plo, phi, hf, hs, lf, ls):
            face_lo = rotate(jnp.where(lower, u[hf], plo), 4, 1)
            next_lo = jnp.where(lower, plo, rotate(u[hs], 4, 1))
            face_hi = rotate(jnp.where(lower, phi, u[lf]), 4, 1)
            next_hi = jnp.where(lower, rotate(u[ls], 4, 1), phi)
            return face_lo, next_lo, face_hi, next_hi

        def from_y(u, h, hf, hs, lf, ls):
            turned = rotate(h, 4, 1)
            face_lo = rotate(jnp.where(ey == 3, turned, u(hf)), 1, 1)
            next_lo = jnp.where(ey == 0, rotate(h, 6, 1), rotate(u(hs), 1, 1))
            face_hi = rotate(jnp.where(ey == 0, turned, u(lf)), 7, 1)
            next_hi = jnp.where(ey == 3, rotate(h, 2, 1), rotate(u(ls), 7, 1))
            return face_lo, next_lo, face_hi, next_hi

        def gather_send(it):
            u = raw[it].reshape(8, 8, 8, 128)
            store_packed(gs.at[it], pack(u, IN), SIDE)
            own = [raw[it, k] for k in range(64)]
            edge = [gs[it, k] for k in range(IN.packed)]
            gs[it, IN.z_hi] = lane_pack(own, True)
            gs[it, IN.z_hi + 1] = lane_pack(edge, True)
            gs[it, IN.z_lo] = lane_pack(own, False)
            gs[it, IN.z_lo + 1] = lane_pack(edge, False)

        def gather_receive(it):
            def put(tile, i, j, value):
                ug[tile, i, j] = value

            receive(gr.at[it], IN, put)
            ug[0, 0:8, 0:8] = raw[it].reshape(8, 8, 8, 128)
            for tile in range(2):
                u = [ug[tile, i] for i in range(10)]
                face_lo, next_lo, face_hi, next_hi = from_x(u, u[8], u[9], 7, 6, 0, 1)
                wide = [next_lo, u[0] + face_lo] + u[1:7]
                wide += [(u[7] + face_hi) * x_mask, next_hi]
                for i in range(10):
                    w = wide[i]
                    face_lo, next_lo, face_hi, next_hi = from_y(
                        lambda j: w[j : j + 1], w[8:9], 7, 6, 0, 1
                    )
                    e[tile, i, 0:1] = next_lo
                    e[tile, i, 1:2] = w[0:1] + face_lo
                    e[tile, i, 2:8] = w[1:7]
                    e[tile, i, 8:9] = w[7:8] + face_hi
                    e[tile, i, 9:10] = next_hi
                x[it, tile] = e[tile, 1:9, 1:9].reshape(64, 8, 128)

        def halves(v, even, odd):
            plus = [v[a] + v[9 - a] for a in range(5)]
            minus = [v[a] - v[9 - a] for a in range(5)]
            out = []
            for k in range(10):
                part = plus if k % 2 == 0 else minus
                total = part[0] * float(SINE[0, k])
                for a in range(1, 5):
                    total = total + part[a] * float(SINE[a, k])
                out.append(total)
            return out

        def unhalves(f):
            first, last = [], []
            for a in range(5):
                even = f[0] * float(SINE[a, 0])
                odd = f[1] * float(SINE[a, 1])
                for k in range(1, 5):
                    even = even + f[2 * k] * float(SINE[a, 2 * k])
                    odd = odd + f[2 * k + 1] * float(SINE[a, 2 * k + 1])
                first.append(even + odd)
                last.append(even - odd)
            return first + last[::-1]

        def boxes(it):
            wide = jnp.concatenate(
                [e[0].reshape(800, 128), e[1].reshape(800, 128)], axis=1
            )
            modes = jnp.dot(wide, fwd_ref[...], precision=lax.Precision.HIGHEST,
                            preferred_element_type=F32)
            sp[0] = modes[:, :128].reshape(10, 10, 8, 128)
            sp[1] = modes[:, 128:].reshape(10, 10, 8, 128)

            def along_x(j, carry):
                for tile in range(2):
                    out = halves([sp[tile, i, j] for i in range(10)], None, None)
                    for i in range(10):
                        sp[tile, i, j] = out[i]
                return carry

            def middle(i, total):
                for tile in range(2):
                    f = halves([sp[tile, i, j] for j in range(10)], None, None)
                    scale = icb[tile]
                    g = [f[j] * (inv_ref[tile, i, j : j + 1] * scale) for j in range(10)]
                    for j in range(10):
                        total = total + f[j] * g[j]
                    out = unhalves(g)
                    for j in range(10):
                        sp[tile, i, j] = out[j]
                return total

            def back_x(j, carry):
                for tile in range(2):
                    out = unhalves([sp[tile, i, j] for i in range(10)])
                    for i in range(10):
                        sp[tile, i, j] = out[i]
                return carry

            lax.fori_loop(0, 10, along_x, 0)
            acc[2 * it] = lax.fori_loop(0, 10, middle, jnp.zeros((8, 128), F32))
            lax.fori_loop(0, 10, back_x, 0)
            wide = jnp.concatenate(
                [sp[0].reshape(800, 128), sp[1].reshape(800, 128)], axis=1
            )
            back = jnp.dot(wide, bwd_ref[...], precision=lax.Precision.HIGHEST,
                           preferred_element_type=F32)
            sp[0] = back[:, :128].reshape(10, 10, 8, 128)
            sp[1] = back[:, 128:].reshape(10, 10, 8, 128)

        def scatter_send(it):
            store_packed(ss.at[it], pack(sp[0], OUT), BOX)
            store_packed(c1p, pack(sp[1], OUT), BOX)
            own = [sp[1, k // 10, k % 10] for k in range(100)]
            edge = [c1p[k] for k in range(OUT.packed)]
            for base, up in ((OUT.z_hi, True), (OUT.z_lo, False)):
                ss[it, base] = lane_pack(own[:64], up)
                ss[it, base + 1] = lane_pack(own[64:], up)
                ss[it, base + 2] = lane_pack(edge, up)

        def scatter_receive(it):
            def put(tile, i, j, value):
                if tile == 0:
                    us[i, j] = value
                else:
                    us[i, j] = us[i, j] + value

            us[0:10, 0:10] = sp[0]
            later = []
            receive(sr.at[it], OUT, lambda t, i, j, v: put(t, i, j, v) if t == 0
                    else later.append((i, j, v)))
            for i, j, v in later:
                put(1, i, j, v)
            u = [us[i] for i in range(12)]
            face_lo, next_lo, face_hi, next_hi = from_x(u, u[10], u[11], 8, 9, 1, 0)
            fold = [u[1] + face_lo, u[2] + next_lo, u[3], u[4], u[5], u[6],
                    u[7] + next_hi, (u[8] + face_hi) * x_mask]
            for i in range(8):
                w = fold[i]
                last = x_mask if i == 7 else 1.0
                face_lo, next_lo, face_hi, next_hi = from_y(
                    lambda j: w[j : j + 1], w[10:11], 8, 9, 1, 0
                )
                zs[it, 8 * i : 8 * i + 1] = (w[1:2] + face_lo) * last
                zs[it, 8 * i + 1 : 8 * i + 2] = (w[2:3] + next_lo) * last
                zs[it, 8 * i + 2 : 8 * i + 6] = w[3:7] * last
                zs[it, 8 * i + 6 : 8 * i + 7] = (w[7:8] + next_hi) * last
                zs[it, 8 * i + 7 : 8 * i + 8] = (w[8:9] + face_hi) * last

        def derive(v, matrix):
            plus = [v[k] + v[7 - k] for k in range(4)]
            minus = [v[k] - v[7 - k] for k in range(4)]
            first, last = [], []
            for a in range(4):
                even = odd = None
                for k in range(4):
                    p = plus[k] * float(0.5 * (matrix[a, k] + matrix[a, 7 - k]))
                    m = minus[k] * float(0.5 * (matrix[a, k] - matrix[a, 7 - k]))
                    even = p if even is None else even + p
                    odd = m if odd is None else odd + m
                first.append(even + odd)
                last.append(odd - even)
            return first + last[::-1]

        def stiffness(it):
            def over_x(j, carry):
                grad = derive([zs[it, 8 * i + j] for i in range(8)], DERIV)
                flux = [grad[i] * wc[8 * i + j] for i in range(8)]
                out = derive(flux, DERIV.T)
                for i in range(8):
                    raw[it + 1, 8 * i + j] = out[i]
                return carry

            def over_y(i, carry):
                grad = derive([zs[it, 8 * i + j] for j in range(8)], DERIV)
                flux = [grad[j] * wc[8 * i + j] for j in range(8)]
                out = derive(flux, DERIV.T)
                for j in range(8):
                    raw[it + 1, 8 * i + j] = raw[it + 1, 8 * i + j] + out[j]
                return carry

            lax.fori_loop(0, 8, over_x, 0)
            lax.fori_loop(0, 8, over_y, 0)
            field = zs[it].reshape(512, 128)
            grad = jnp.dot(field, der_ref[0], precision=lax.Precision.HIGHEST,
                           preferred_element_type=F32)
            flux = grad * wc[...].reshape(512, 128)
            out = jnp.dot(flux, der_ref[1], precision=lax.Precision.HIGHEST,
                          preferred_element_type=F32)
            total = raw[it + 1].reshape(512, 128) + out
            raw[it + 1] = total.reshape(64, 8, 128)
            acc[2 * it + 1] = jnp.sum((total * field).reshape(64, 8, 128), axis=0)

        rings = ((red_y, ny, gy, ring_y), (red_x, runs, gz // z_run, ring_x),
                 (red_z, ring, gx * z_run + gz % z_run, ring_z))

        def reduce_start(phase, value):
            ref, count, me, to = rings[phase]
            ref[me] = value
            for t in range(1, count):
                pltpu.make_async_remote_copy(
                    src_ref=ref.at[me],
                    dst_ref=ref.at[me],
                    send_sem=rsend.at[phase],
                    recv_sem=rrecv.at[phase],
                    device_id=to(t),
                    device_id_type=MESH,
                ).start()

        def reduce_wait(phase):
            ref, count, _, _ = rings[phase]
            if count > 1:
                part = ref.at[pl.ds(0, count - 1)]
                wait_all(part, rrecv.at[phase])
            return jnp.sum(ref[0:count], axis=0)

        def reduce_end(phase):
            ref, count, _, _ = rings[phase]
            if count > 1:
                wait_all(ref.at[pl.ds(0, count - 1)], rsend.at[phase])

        def relaid(ref, store):
            for i in range(8):
                for ex in range(2):
                    rows[i * 64 + ex * 32 : i * 64 + ex * 32 + 32] = ref[ex * 8 + i]
            for i in range(8):
                for j in range(8):
                    store(8 * i + j, rows[pl.ds(i * 64 + j, 8, stride=8), :])

        def put_b(k, value):
            raw[0, k] = value

        def put_c(k, value):
            zs[0, k] = value

        relaid(b_ref, put_b)
        relaid(c_ref, put_c)
        mean = jnp.dot(jnp.sum(zs[0], axis=0), mean_ref[...], precision=lax.Precision.HIGHEST,
                       preferred_element_type=F32)
        icb[0] = 1.0 / mean[:, :128]
        icb[1] = 1.0 / mean[:, 128:]
        for i in range(8):
            wc[8 * i : 8 * i + 8] = zs[0, 8 * i : 8 * i + 8] * (wyz_ref[...] * float(WEIGHTS[i]))

        def step(it, carry):
            gather_send(it)

            @pl.when(it == 0)
            def _():
                pl.semaphore_wait(barrier, len(partners))

            send(gs.at[it], gr.at[it], IN, gsend.at[it], grecv.at[it])
            wait_all(gr.at[it], grecv.at[it])
            gather_receive(it)
            boxes(it)
            scatter_send(it)
            send(ss.at[it], sr.at[it], OUT, ssend.at[it], srecv.at[it])
            wait_all(sr.at[it], srecv.at[it])
            scatter_receive(it)
            stiffness(it)
            return carry

        lax.fori_loop(0, 2, step, 0)
        local = jnp.zeros((8, 128), F32)
        for k in range(4):
            local = jnp.where(sub == k, jnp.sum(acc[k], axis=(0, 1), keepdims=True), local)
        reduce_start(0, local)
        gather_send(2)
        send(gs.at[2], gr.at[2], IN, gsend.at[2], grecv.at[2])
        reduce_start(1, reduce_wait(0))
        reduce_start(2, reduce_wait(1))
        wait_all(gr.at[2], grecv.at[2])
        gather_receive(2)
        sums = reduce_wait(2)
        rho, delta, gamma, eps = (sums[k : k + 1] for k in range(4))
        a0 = rho / delta
        rz = a0 * a0 * gamma - rho
        up = 1.0 + rz / rho
        curve = up * up * delta - 2.0 * a0 * up * gamma + a0 * a0 * eps
        a1 = rz / curve
        first = a0 + a1 * up
        second = a1 * a0

        def write(values, ref):
            for k in range(64):
                rows[pl.ds((k // 8) * 64 + k % 8, 8, stride=8), :] = values[k]
            for i in range(8):
                for ex in range(2):
                    ref[ex * 8 + i] = rows[i * 64 + ex * 32 : i * 64 + ex * 32 + 32]

        write(zs[0] * first - zs[1] * second, sol_ref)
        mixed = x[0] - x[1] * first + x[2] * second
        wide = jnp.concatenate(
            [mixed[0].reshape(512, 128), mixed[1].reshape(512, 128)], axis=1
        )
        out = jnp.dot(wide, asm_ref[...], precision=lax.Precision.HIGHEST,
                      preferred_element_type=F32)
        write(out.reshape(64, 8, 128), res_ref)
        for it in range(3):
            wait_all(gr.at[it], gsend.at[it])
        for it in range(2):
            wait_all(sr.at[it], ssend.at[it])
        for phase in range(3):
            reduce_end(phase)

    return kernel


def solution(mesh):
    sizes = tuple(mesh.shape[a] for a in AXES)
    z_run = 4 if sizes[2] % 4 == 0 else sizes[2]
    ring = sizes[0] * z_run
    forward, assemble = z_tables(16)
    der = np.kron(np.eye(16), DERIV)
    inverse = np.zeros((2, 10, 10, 128))
    tiled = np.tile(INVERSE, (1, 1, 16))
    inverse[0] = tiled[:, :, :128]
    inverse[1, :, :, :32] = tiled[:, :, 128:]
    mean = np.zeros((128, 256))
    mean[:, :160] = np.kron(np.eye(16), np.ones((8, 10))) / SIDE**3
    mean[0, 160:] = 1.0
    wyz = np.broadcast_to(
        WEIGHTS[:, None, None] * np.tile(WEIGHTS, 16)[None, None, :], (8, 8, 128)
    )
    tables = [
        jnp.asarray(t, F32)
        for t in (wyz, forward, forward.T, assemble, np.stack([der.T, der]), inverse, mean)
    ]
    vmem = pl.BlockSpec(memory_space=pltpu.VMEM)
    dma = pltpu.SemaphoreType.DMA

    def block(*shape):
        return pltpu.VMEM(shape + (8, 128), F32)

    call = pl.pallas_call(
        make_kernel(sizes, z_run),
        out_shape=[jax.ShapeDtypeStruct((16, 32, 128), F32)] * 2,
        in_specs=[vmem] * 9,
        out_specs=[vmem] * 2,
        scratch_shapes=[
            pltpu.VMEM((512, 128), F32),
            block(3, 64), block(64), block(2),
            block(3, IN.total), block(3, IN.received), block(2, 10, 9), block(2, 10, 10),
            block(3, 2, 64), block(2, 10, 10), block(OUT.packed),
            block(2, OUT.total), block(2, OUT.received), block(12, 11),
            block(2, 64), block(4),
            block(sizes[1]), block(sizes[2] // z_run), block(ring),
            dma((3,)), dma((3,)), dma((2,)), dma((2,)), dma((3,)), dma((3,)),
        ],
        compiler_params=pltpu.CompilerParams(
            collective_id=0, has_side_effects=True, vmem_limit_bytes=48 * 1024 * 1024
        ),
    )

    def shards(right_side, coefficient):
        return tuple(call(right_side, coefficient, *tables))

    spec = P(*AXES)
    return jax.shard_map(
        shards, mesh=mesh, in_specs=(spec, spec), out_specs=(spec, spec), check_vma=False
    )
```

time: 797 us -> 99.9 us (0.13)
  blocking collectives: 368 us -> 0 us
  starting transfers between devices: 213 us -> 0 us
  waiting for transfers between devices: 115 us -> 0 us
  Pallas kernels: 0 us -> 89.3 us
  local copies, waits for them, and re-layouts: 43 us -> 9.58 us
  matrix products: 23.5 us -> 0 us
  other arithmetic: 20.7 us -> 0 us
    psum x3 -> x0, blocking collectives: 368 us -> none  [inner_sum(): return lax.psum(jnp.sum(multiplicity * first * second), ('gx', 'gy', 'gz'))]
    ppermute x54 -> x0, starting transfers between devices: 213 us -> none  [the longest x27 149 us: extended(): lax.ppermute(tail, axis, [(i, (i + 1) % count) for i in range(ends)])]
    ppermute x54 -> x0, waiting for transfers between devices: 115 us -> none  [the longest x27 92.1 us: extended(): lax.ppermute(head, axis, [((i + 1) % count, i) for i in range(ends)])]
    pallas_call x0 -> x1, Pallas kernels: none -> 89.3 us  [shards(): return tuple(call(right_side, coefficient, *tables))]
    dot_general x24 -> x0, matrix products: 23.5 us -> none  [the longest x16 17.1 us: contract_first(): jnp.einsum('ij,aj...->ai...', matrix, shaped, precision=HIGHEST_MODE)]
    slice x60 -> x0, local copies, waits for them, and re-layouts: 18.6 us -> none  [the longest x4 5.11 us: gather_boxes_first(): left_part = field[0:per_side * elements:per_side][:, None]]
  transfers between devices with their start and end apart: 54 -> 0, of which waited for: 34 -> 0; matrix products, arithmetic and copies ran while one was open for 1% -> 0% of each run, Pallas kernels for 0% -> 0%
where the time goes in v1:
time: 99.9 us; the launch traced here: 99.6 us
  Pallas kernels  89.3 us (89%)
  local copies, waits for them, and re-layouts  9.58 us (10%)
    pallas_call x1, Pallas kernels, shards(): return tuple(call(right_side, coefficient, *tables))  89.3 us
    unnamed x20, local copies, waits for them, and re-layouts  9.58 us

profile of v1, /device:TPU:1, one launch (start us, length us, event | category | flops | bytes accessed | tf_op | source)
XLA Modules:
  0.0 99.6 jit_solution(16678361584789747543)
XLA Ops:
  0.6 0.0 copy-start
  0.6 0.9 copy-done
  1.6 0.0 copy-start.1
  1.6 0.9 copy-done.1
  2.5 0.0 copy-start.2
  2.5 0.9 copy-done.2
  3.5 0.0 copy-start.3
  3.5 0.9 copy-done.3
  4.4 0.0 copy-start.4
  4.4 0.9 copy-done.4
  5.3 0.0 copy-start.5
  5.4 0.9 copy-done.5
  6.3 0.0 copy-start.6
  6.3 0.9 copy-done.6
  7.2 0.0 copy-start.7
  7.2 0.9 copy-done.7
  8.1 0.0 copy-start.8
  8.1 0.8 copy-done.8
  8.8 89.3 %shard_map.104 = (f32[16,32,128]{2,1,0:T(8,128)S(1)}, f32[16,32,128]{2,1,0:T(8,128)S(1)}) custom-call(f32[16,32,128]{2,1,0:T(8,128)S(1)} %copy-done, f32[16,32,128]{2,1,0:T(8,128)S(1)} %copy-done.1, f32[8,8,128]{2,1,0:T(8,128)S(1)} %copy-done.8, f32[256,256]{1,0:T(8,128)S(1)} %copy-done.3, f32[256,256]{1,0:T(8,128)S(1)} %copy-done.2, ...), custom_call_target="tpu_custom_call" | custom-call | tf_op jit(solution)/shard_map/pallas_call | solution.py:622
  98.2 0.7 copy.13
  98.9 0.7 copy.14
Async XLA Ops:
  0.6 1.0 copy-start
  1.6 0.9 copy-start.1
  2.5 0.9 copy-start.2
  3.5 0.9 copy-start.3
  4.4 0.9 copy-start.4
  5.3 0.9 copy-start.5
  6.3 0.9 copy-start.6
  7.2 0.9 copy-start.7
  8.1 0.8 copy-start.8

commit v2 on v1

--- a/solution.py
+++ b/solution.py
@@ -14,7 +14,11 @@
 AXES = ("gx", "gy", "gz")
 MESH = pl.DeviceIdType.MESH
 F32 = jnp.float32
-NEAR = [o for o in itertools.product((-1, 0, 1), repeat=3) if o != (0, 0, 0)]
+NEAR = sorted(
+    (o for o in itertools.product((-1, 0, 1), repeat=3) if o != (0, 0, 0)),
+    key=lambda o: [(1, 1, 1), (1, 0, 1), (1, 1, 0), (0, 1, 1), (0, 0, 1), (1, 0, 0),
+                   (0, 1, 0)].index(tuple(map(abs, o))),
+)
 
 
 def legendre_rows(points, degree):
@@ -94,27 +98,31 @@
 class Halo:
     def __init__(self, n, hf, hs, lf, ls):
         self.n, self.hf, self.hs, self.lf, self.ls = n, hf, hs, lf, ls
-        self.packed = 4 * n + 4
         self.own_z = -(-n * n // 64)
-        self.z_hi = self.packed
-        self.z_lo = self.packed + self.own_z + 1
-        self.total = self.packed + 2 * (self.own_z + 1)
-        self.slot, at = {}, 0
+        self.corner = 4 * n
+        self.z_part = {1: 4 * n + 4, -1: 4 * n + 7 + self.own_z}
+        self.total = 4 * n + 10 + 2 * self.own_z
+        self.slot, at, height = {}, 0, 0
         for o in NEAR:
-            self.slot[o] = (at, self.part(o)[1])
-            at += self.part(o)[1]
+            _, count, tall = self.part(o)
+            self.slot[o] = at
+            at += count
+            height += count * tall
         self.received = at
+        self.vectors = height // 8
 
     def part(self, o):
         n = self.n
         if o[2]:
-            base = self.z_hi if o[2] > 0 else self.z_lo
-            return (base, self.own_z) if o[:2] == (0, 0) else (base + self.own_z, 1)
+            base = self.z_part[o[2]]
+            if o[0]:
+                return (base + self.own_z + (1 if o[0] > 0 else 2), 1, 2)
+            return (base + self.own_z, 1, 8) if o[1] else (base, self.own_z, 8)
         if o[0] == 0:
-            return (0 if o[1] > 0 else n, n)
+            return (0 if o[1] > 0 else n, n, 8)
         if o[1] == 0:
-            return (2 * n if o[0] > 0 else 3 * n, n)
-        return (4 * n + {(1, 1): 0, (1, -1): 1, (-1, 1): 2, (-1, -1): 3}[o[:2]], 1)
+            return (2 * n if o[0] > 0 else 3 * n, n, 8)
+        return (4 * n + [(1, 1), (1, -1), (-1, 1), (-1, -1)].index(o[:2]), 1, 4)
 
 
 IN = Halo(SIDE, 7, 6, 0, 1)
@@ -127,10 +135,11 @@
     runs = nz // z_run
     ring = nx * z_run
 
-    def kernel(b_ref, c_ref, wyz_ref, fwd_ref, bwd_ref, asm_ref, der_ref, inv_ref, mean_ref,
-               sol_ref, res_ref,
-               rows, raw, wc, icb, gs, gr, ug, e, x, sp, c1p, ss, sr, us, zs, acc,
-               red_y, red_x, red_z, gsend, grecv, ssend, srecv, rsend, rrecv):
+    def kernel(b_ref, c_ref, *rest):
+        tables, rest = rest[:7], rest[7:]
+        (sol_ref, res_ref, b_rows, c_rows, wyz_ref, fwd_ref, bwd_ref, asm_ref, der_ref, inv_ref,
+         mean_ref, raw, wc, icb, gs, gr, ug, e, x, sp, ss, sr, us, zs, acc,
+         red_y, red_x, red_z, gsend, grecv, ssend, srecv, rsend, rrecv, load) = rest
         gx, gy, gz = (lax.axis_index(a) for a in AXES)
 
         def near(o):
@@ -153,6 +162,19 @@
         barrier = pltpu.get_barrier_semaphore()
         for device in partners:
             pl.semaphore_signal(barrier, inc=1, device_id=device, device_id_type=MESH)
+
+        loads = []
+        for source, target in ((b_ref, b_rows), (c_ref, c_rows)):
+            for ex in range(2):
+                loads.append((source.at[pl.ds(8 * ex, 8)], target.at[:, pl.ds(32 * ex, 32)]))
+        kept = (wyz_ref, fwd_ref, bwd_ref, asm_ref, der_ref, inv_ref, mean_ref)
+        loads += list(zip(tables, kept))
+        loads = [
+            pltpu.make_async_copy(source, target, load.at[k])
+            for k, (source, target) in enumerate(loads)
+        ]
+        for copy in loads:
+            copy.start()
 
         sub = lax.broadcasted_iota(jnp.int32, (8, 128), 0)
         lane = lax.broadcasted_iota(jnp.int32, (8, 128), 1)
@@ -186,8 +208,12 @@
         def store_packed(ref, parts, n):
             for k in range(4):
                 ref[k * n : (k + 1) * n] = parts[k]
-            for k in range(4):
-                ref[4 * n + k] = parts[4][k]
+            for k, corner in enumerate(parts[4]):
+                if k % 2 == 0:
+                    corner = jnp.where(sub < 2, rotate(corner, 2, 0), corner)
+                else:
+                    corner = jnp.where(sub < 2, corner, rotate(corner, 6, 0))
+                ref[4 * n + k, 0:4] = corner[0:4]
 
         def lane_pack(values, up):
             total = None
@@ -196,13 +222,33 @@
                 total = moved if total is None else jnp.where(pair == k, moved, total)
             return total
 
+        def fan(value, sign):
+            turned = value
+            for k in range(1, 4):
+                turned = jnp.where(ey == k, rotate(value, sign * 32 * k, 1), turned)
+            return turned
+
+        def store_lanes(ref, own, parts, halo):
+            for up, base in ((True, halo.z_part[1]), (False, halo.z_part[-1])):
+                for k in range(halo.own_z):
+                    ref[base + k] = lane_pack(own[64 * k : 64 * k + 64], up)
+                n, at = halo.n, base + halo.own_z
+                planes = [parts[side][k] for side in (0, 1) for k in range(n)]
+                ref[at] = lane_pack(planes, up)
+                for k in range(2):
+                    planes = [parts[2 + k][j] for j in range(n)] + parts[4][2 * k : 2 * k + 2]
+                    moved = fan(lane_pack(planes, up), 1)
+                    moved = jnp.where(lane // 32 == ey, moved, 0.0)
+                    ref[at + 1 + k, 0:1] = jnp.sum(moved[0:4], axis=0, keepdims=True)
+                    ref[at + 1 + k, 1:2] = jnp.sum(moved[4:8], axis=0, keepdims=True)
+
         def send(src, dst, halo, send_sem, recv_sem):
             for o in NEAR:
-                at, count = halo.part(o)
-                to, _ = halo.slot[(-o[0], -o[1], -o[2])]
+                at, count, tall = halo.part(o)
+                to = halo.slot[(-o[0], -o[1], -o[2])]
                 pltpu.make_async_remote_copy(
-                    src_ref=src.at[pl.ds(at, count)],
-                    dst_ref=dst.at[pl.ds(to, count)],
+                    src_ref=src.at[pl.ds(at, count), pl.ds(0, tall)],
+                    dst_ref=dst.at[pl.ds(to, count), pl.ds(0, tall)],
                     send_sem=send_sem,
                     recv_sem=recv_sem,
                     device_id=near(o),
@@ -212,19 +258,28 @@
         def wait_all(ref, sem):
             pltpu.make_async_copy(ref, ref, sem).wait()
 
-        def merged_lanes(dst, halo, dz):
-            n = halo.n
-
-            def got(dx, dy):
-                return dst[halo.slot[(dx, dy, dz)][0]]
-
-            out = jnp.where(ey >= 2, got(0, -1), rotate(got(0, 1), -2 * n, 1))
-            out = jnp.where(pair >= 2 * n, got(-1, 0), out)
-            out = jnp.where(pair >= 3 * n, got(1, 0), out)
-            low = jnp.where(ey >= 2, got(-1, -1), rotate(got(-1, 1), -2, 1))
-            high = jnp.where(ey >= 2, got(1, -1), rotate(got(1, 1), -2, 1))
-            out = jnp.where(pair >= 4 * n, low, out)
-            return jnp.where(pair >= 4 * n + 2, high, out)
+        def wait_halo(ref, halo, sem):
+            wait_all(ref.at[pl.ds(0, halo.vectors)], sem)
+
+        def y_lanes(dst, halo, dz):
+            low, high = dst[halo.slot[(0, -1, dz)]], dst[halo.slot[(0, 1, dz)]]
+            return jnp.where(ey >= 2, low, rotate(high, -2 * halo.n, 1))
+
+        def x_lanes(dst, halo, dx, dz):
+            def got(dy):
+                at = halo.slot[(dx, dy, dz)]
+                value = jnp.where(lower, dst[at, 0:1], dst[at, 1:2])
+                return fan(value, -1)
+
+            corner = jnp.where(ey >= 2, got(-1), rotate(got(1), -2, 1))
+            return jnp.where(pair >= halo.n, corner, got(0))
+
+        def xy_corner(dst, halo, dx):
+            low, high = dst[halo.slot[(dx, -1, 0)], 0:4], dst[halo.slot[(dx, 1, 0)], 0:4]
+            low, high = jnp.concatenate([low, low], 0), jnp.concatenate([high, high], 0)
+            low = jnp.where(lower, low, rotate(low, 2, 0))
+            high = jnp.where(lower, high, rotate(high, 6, 0))
+            return jnp.where(ey >= 2, low, high)
 
         def unlane(low, high, k):
             return z_mask * jnp.where(
@@ -235,26 +290,28 @@
             n = halo.n
 
             def at(o, k=0):
-                return dst[halo.slot[o][0] + k]
-
-            own_lo = [dst[halo.slot[(0, 0, -1)][0] + k] for k in range(halo.own_z)]
-            own_hi = [dst[halo.slot[(0, 0, 1)][0] + k] for k in range(halo.own_z)]
+                return dst[halo.slot[o] + k]
+
+            own_lo = [dst[halo.slot[(0, 0, -1)] + k] for k in range(halo.own_z)]
+            own_hi = [dst[halo.slot[(0, 0, 1)] + k] for k in range(halo.own_z)]
             for i in range(n):
                 for j in range(n):
                     k = i * n + j
                     put(1, i, j, unlane(own_lo[k // 64], own_hi[k // 64], k % 64))
-            low, high = merged_lanes(dst, halo, -1), merged_lanes(dst, halo, 1)
+            low, high = y_lanes(dst, halo, -1), y_lanes(dst, halo, 1)
+            below = x_lanes(dst, halo, -1, -1), x_lanes(dst, halo, -1, 1)
+            above = x_lanes(dst, halo, 1, -1), x_lanes(dst, halo, 1, 1)
             for k in range(n):
                 put(0, k, n, y_mask * jnp.where(ey >= 2, at((0, -1, 0), k), at((0, 1, 0), k)))
                 put(1, k, n, y_mask * unlane(low, high, k))
                 put(0, n, k, fx_lo * at((-1, 0, 0), k))
-                put(1, n, k, fx_lo * unlane(low, high, 2 * n + k))
+                put(1, n, k, fx_lo * unlane(*below, k))
                 put(0, n + 1, k, fx_hi * at((1, 0, 0), k))
-                put(1, n + 1, k, fx_hi * unlane(low, high, 3 * n + k))
-            put(0, n, n, fx_lo * y_mask * jnp.where(ey >= 2, at((-1, -1, 0)), at((-1, 1, 0))))
-            put(1, n, n, fx_lo * y_mask * unlane(low, high, 4 * n))
-            put(0, n + 1, n, fx_hi * y_mask * jnp.where(ey >= 2, at((1, -1, 0)), at((1, 1, 0))))
-            put(1, n + 1, n, fx_hi * y_mask * unlane(low, high, 4 * n + 2))
+                put(1, n + 1, k, fx_hi * unlane(*above, k))
+            put(0, n, n, fx_lo * y_mask * xy_corner(dst, halo, -1))
+            put(1, n, n, fx_lo * y_mask * unlane(*below, n))
+            put(0, n + 1, n, fx_hi * y_mask * xy_corner(dst, halo, 1))
+            put(1, n + 1, n, fx_hi * y_mask * unlane(*above, n))
 
         def from_x(u, plo, phi, hf, hs, lf, ls):
             face_lo = rotate(jnp.where(lower, u[hf], plo), 4, 1)
@@ -273,13 +330,10 @@
 
         def gather_send(it):
             u = raw[it].reshape(8, 8, 8, 128)
-            store_packed(gs.at[it], pack(u, IN), SIDE)
-            own = [raw[it, k] for k in range(64)]
-            edge = [gs[it, k] for k in range(IN.packed)]
-            gs[it, IN.z_hi] = lane_pack(own, True)
-            gs[it, IN.z_hi + 1] = lane_pack(edge, True)
-            gs[it, IN.z_lo] = lane_pack(own, False)
-            gs[it, IN.z_lo + 1] = lane_pack(edge, False)
+            parts = pack(u, IN)
+            store_packed(gs.at[it], parts, SIDE)
+            store_lanes(gs.at[it], [raw[it, k] for k in range(64)], parts, IN)
+            send(gs.at[it], gr.at[it], IN, gsend.at[it], grecv.at[it])
 
         def gather_receive(it):
             def put(tile, i, j, value):
@@ -332,7 +386,7 @@
             wide = jnp.concatenate(
                 [e[0].reshape(800, 128), e[1].reshape(800, 128)], axis=1
             )
-            modes = jnp.dot(wide, fwd_ref[...], precision=lax.Precision.HIGHEST,
+            modes = jnp.dot(wide, fwd_ref[...], precision=lax.Precision.HIGH,
                             preferred_element_type=F32)
             sp[0] = modes[:, :128].reshape(10, 10, 8, 128)
             sp[1] = modes[:, 128:].reshape(10, 10, 8, 128)
@@ -369,20 +423,16 @@
             wide = jnp.concatenate(
                 [sp[0].reshape(800, 128), sp[1].reshape(800, 128)], axis=1
             )
-            back = jnp.dot(wide, bwd_ref[...], precision=lax.Precision.HIGHEST,
+            back = jnp.dot(wide, bwd_ref[...], precision=lax.Precision.HIGH,
                            preferred_element_type=F32)
             sp[0] = back[:, :128].reshape(10, 10, 8, 128)
             sp[1] = back[:, 128:].reshape(10, 10, 8, 128)
 
         def scatter_send(it):
             store_packed(ss.at[it], pack(sp[0], OUT), BOX)
-            store_packed(c1p, pack(sp[1], OUT), BOX)
             own = [sp[1, k // 10, k % 10] for k in range(100)]
-            edge = [c1p[k] for k in range(OUT.packed)]
-            for base, up in ((OUT.z_hi, True), (OUT.z_lo, False)):
-                ss[it, base] = lane_pack(own[:64], up)
-                ss[it, base + 1] = lane_pack(own[64:], up)
-                ss[it, base + 2] = lane_pack(edge, up)
+            store_lanes(ss.at[it], own, pack(sp[1], OUT), OUT)
+            send(ss.at[it], sr.at[it], OUT, ssend.at[it], srecv.at[it])
 
         def scatter_receive(it):
             def put(tile, i, j, value):
@@ -448,10 +498,10 @@
             lax.fori_loop(0, 8, over_x, 0)
             lax.fori_loop(0, 8, over_y, 0)
             field = zs[it].reshape(512, 128)
-            grad = jnp.dot(field, der_ref[0], precision=lax.Precision.HIGHEST,
+            grad = jnp.dot(field, der_ref[0], precision=lax.Precision.HIGH,
                            preferred_element_type=F32)
             flux = grad * wc[...].reshape(512, 128)
-            out = jnp.dot(flux, der_ref[1], precision=lax.Precision.HIGHEST,
+            out = jnp.dot(flux, der_ref[1], precision=lax.Precision.HIGH,
                           preferred_element_type=F32)
             total = raw[it + 1].reshape(512, 128) + out
             raw[it + 1] = total.reshape(64, 8, 128)
@@ -462,11 +512,11 @@
 
         def reduce_start(phase, value):
             ref, count, me, to = rings[phase]
-            ref[me] = value
+            ref[me, 0:1] = value
             for t in range(1, count):
                 pltpu.make_async_remote_copy(
-                    src_ref=ref.at[me],
-                    dst_ref=ref.at[me],
+                    src_ref=ref.at[me, pl.ds(0, 1)],
+                    dst_ref=ref.at[me, pl.ds(0, 1)],
                     send_sem=rsend.at[phase],
                     recv_sem=rrecv.at[phase],
                     device_id=to(t),
@@ -476,22 +526,18 @@
         def reduce_wait(phase):
             ref, count, _, _ = rings[phase]
             if count > 1:
-                part = ref.at[pl.ds(0, count - 1)]
-                wait_all(part, rrecv.at[phase])
-            return jnp.sum(ref[0:count], axis=0)
+                wait_all(ref.at[pl.ds(0, count - 1), pl.ds(0, 1)], rrecv.at[phase])
+            return jnp.sum(ref[0:count, 0:1], axis=0)
 
         def reduce_end(phase):
             ref, count, _, _ = rings[phase]
             if count > 1:
-                wait_all(ref.at[pl.ds(0, count - 1)], rsend.at[phase])
+                wait_all(ref.at[pl.ds(0, count - 1), pl.ds(0, 1)], rsend.at[phase])
 
         def relaid(ref, store):
             for i in range(8):
-                for ex in range(2):
-                    rows[i * 64 + ex * 32 : i * 64 + ex * 32 + 32] = ref[ex * 8 + i]
-            for i in range(8):
                 for j in range(8):
-                    store(8 * i + j, rows[pl.ds(i * 64 + j, 8, stride=8), :])
+                    store(8 * i + j, ref[i, pl.ds(j, 8, stride=8), :])
 
         def put_b(k, value):
             raw[0, k] = value
@@ -499,8 +545,14 @@
         def put_c(k, value):
             zs[0, k] = value
 
-        relaid(b_ref, put_b)
-        relaid(c_ref, put_c)
+        loads[0].wait()
+        loads[1].wait()
+        relaid(b_rows, put_b)
+        pl.semaphore_wait(barrier, len(partners))
+        gather_send(0)
+        for copy in loads[2:]:
+            copy.wait()
+        relaid(c_rows, put_c)
         mean = jnp.dot(jnp.sum(zs[0], axis=0), mean_ref[...], precision=lax.Precision.HIGHEST,
                        preferred_element_type=F32)
         icb[0] = 1.0 / mean[:, :128]
@@ -509,36 +561,32 @@
             wc[8 * i : 8 * i + 8] = zs[0, 8 * i : 8 * i + 8] * (wyz_ref[...] * float(WEIGHTS[i]))
 
         def step(it, carry):
-            gather_send(it)
-
-            @pl.when(it == 0)
-            def _():
-                pl.semaphore_wait(barrier, len(partners))
-
-            send(gs.at[it], gr.at[it], IN, gsend.at[it], grecv.at[it])
-            wait_all(gr.at[it], grecv.at[it])
+            wait_halo(gr.at[it], IN, grecv.at[it])
             gather_receive(it)
             boxes(it)
             scatter_send(it)
-            send(ss.at[it], sr.at[it], OUT, ssend.at[it], srecv.at[it])
-            wait_all(sr.at[it], srecv.at[it])
+            wait_halo(sr.at[it], OUT, srecv.at[it])
             scatter_receive(it)
             stiffness(it)
+
+            @pl.when(it == 1)
+            def _():
+                local = jnp.zeros((1, 128), F32)
+                for k in range(4):
+                    total = jnp.sum(acc[k], axis=(0, 1), keepdims=True)
+                    local = jnp.where(lane[0:1] == k, total, local)
+                reduce_start(0, local)
+
+            gather_send(it + 1)
             return carry
 
         lax.fori_loop(0, 2, step, 0)
-        local = jnp.zeros((8, 128), F32)
-        for k in range(4):
-            local = jnp.where(sub == k, jnp.sum(acc[k], axis=(0, 1), keepdims=True), local)
-        reduce_start(0, local)
-        gather_send(2)
-        send(gs.at[2], gr.at[2], IN, gsend.at[2], grecv.at[2])
         reduce_start(1, reduce_wait(0))
         reduce_start(2, reduce_wait(1))
-        wait_all(gr.at[2], grecv.at[2])
+        wait_halo(gr.at[2], IN, grecv.at[2])
         gather_receive(2)
         sums = reduce_wait(2)
-        rho, delta, gamma, eps = (sums[k : k + 1] for k in range(4))
+        rho, delta, gamma, eps = (sums[:, k : k + 1] for k in range(4))
         a0 = rho / delta
         rz = a0 * a0 * gamma - rho
         up = 1.0 + rz / rho
@@ -549,23 +597,23 @@
 
         def write(values, ref):
             for k in range(64):
-                rows[pl.ds((k // 8) * 64 + k % 8, 8, stride=8), :] = values[k]
-            for i in range(8):
                 for ex in range(2):
-                    ref[ex * 8 + i] = rows[i * 64 + ex * 32 : i * 64 + ex * 32 + 32]
+                    ref[8 * ex + k // 8, pl.ds(k % 8, 4, stride=8), :] = values[
+                        k, 4 * ex : 4 * ex + 4
+                    ]
 
         write(zs[0] * first - zs[1] * second, sol_ref)
         mixed = x[0] - x[1] * first + x[2] * second
         wide = jnp.concatenate(
             [mixed[0].reshape(512, 128), mixed[1].reshape(512, 128)], axis=1
         )
-        out = jnp.dot(wide, asm_ref[...], precision=lax.Precision.HIGHEST,
+        out = jnp.dot(wide, asm_ref[...], precision=lax.Precision.HIGH,
                       preferred_element_type=F32)
         write(out.reshape(64, 8, 128), res_ref)
         for it in range(3):
-            wait_all(gr.at[it], gsend.at[it])
+            wait_halo(gr.at[it], IN, gsend.at[it])
         for it in range(2):
-            wait_all(sr.at[it], ssend.at[it])
+            wait_halo(sr.at[it], OUT, ssend.at[it])
         for phase in range(3):
             reduce_end(phase)
 
@@ -601,17 +649,18 @@
     call = pl.pallas_call(
         make_kernel(sizes, z_run),
         out_shape=[jax.ShapeDtypeStruct((16, 32, 128), F32)] * 2,
-        in_specs=[vmem] * 9,
+        in_specs=[pl.BlockSpec(memory_space=pltpu.HBM)] * 9,
         out_specs=[vmem] * 2,
         scratch_shapes=[
-            pltpu.VMEM((512, 128), F32),
+            pltpu.VMEM((8, 64, 128), F32), pltpu.VMEM((8, 64, 128), F32),
+            *[pltpu.VMEM(t.shape, F32) for t in tables],
             block(3, 64), block(64), block(2),
             block(3, IN.total), block(3, IN.received), block(2, 10, 9), block(2, 10, 10),
-            block(3, 2, 64), block(2, 10, 10), block(OUT.packed),
+            block(3, 2, 64), block(2, 10, 10),
             block(2, OUT.total), block(2, OUT.received), block(12, 11),
             block(2, 64), block(4),
             block(sizes[1]), block(sizes[2] // z_run), block(ring),
-            dma((3,)), dma((3,)), dma((2,)), dma((2,)), dma((3,)), dma((3,)),
+            dma((3,)), dma((3,)), dma((2,)), dma((2,)), dma((3,)), dma((3,)), dma((11,)),
         ],
         compiler_params=pltpu.CompilerParams(
             collective_id=0, has_side_effects=True, vmem_limit_bytes=48 * 1024 * 1024

time: 99.9 us -> 84.7 us (0.85)
  Pallas kernels: 89.3 us -> 74.1 us
    pallas_call x1, Pallas kernels: 89.3 us -> 74.1 us  [shards(): return tuple(call(right_side, coefficient, *tables))]
where the time goes in v2:
time: 84.7 us; the launch traced here: 84.3 us
  Pallas kernels  74.1 us (87%)
  local copies, waits for them, and re-layouts  9.58 us (11%)
    pallas_call x1, Pallas kernels, shards(): return tuple(call(right_side, coefficient, *tables))  74.1 us
    unnamed x20, local copies, waits for them, and re-layouts  9.58 us

profile of v2, /device:TPU:1, one launch (start us, length us, event | category | flops | bytes accessed | tf_op | source)
XLA Modules:
  0.0 84.3 jit_solution(968999327918940395)
XLA Ops:
  0.6 0.0 copy-start
  0.6 0.9 %copy-done = f32[16,32,128]{2,1,0:T(8,128)S(1)} copy-done((f32[16,32,128]{2,1,0:T(8,128)S(1)}, f32[16,32,128]{2,1,0:T(8,128)}, u32[]{:S(2)}) %copy-start) | copy-done | bytes 262168
  1.6 0.0 copy-start.1
  1.6 0.9 %copy-done.1 = f32[16,32,128]{2,1,0:T(8,128)S(1)} copy-done((f32[16,32,128]{2,1,0:T(8,128)S(1)}, f32[16,32,128]{2,1,0:T(8,128)}, u32[]{:S(2)}) %copy-start.1) | copy-done | bytes 262168
  2.5 0.0 copy-start.2
  2.5 0.9 %copy-done.2 = f32[256,256]{1,0:T(8,128)S(1)} copy-done((f32[256,256]{1,0:T(8,128)S(1)}, f32[256,256]{1,0:T(8,128)}, u32[]{:S(2)}) %copy-start.2) | copy-done | bytes 262168
  3.5 0.0 copy-start.3
  3.5 0.9 %copy-done.3 = f32[256,256]{1,0:T(8,128)S(1)} copy-done((f32[256,256]{1,0:T(8,128)S(1)}, f32[256,256]{1,0:T(8,128)}, u32[]{:S(2)}) %copy-start.3) | copy-done | bytes 262168
  4.4 0.0 copy-start.4
  4.4 0.9 %copy-done.4 = f32[2,10,10,128]{3,2,1,0:T(8,128)S(1)} copy-done((f32[2,10,10,128]{3,2,1,0:T(8,128)S(1)}, f32[2,10,10,128]{3,2,1,0:T(8,128)}, u32[]{:S(2)}) %copy-start.4) | copy-done | bytes 102424
  5.3 0.0 copy-start.5
  5.4 0.9 %copy-done.5 = f32[128,256]{1,0:T(8,128)S(1)} copy-done((f32[128,256]{1,0:T(8,128)S(1)}, f32[128,256]{1,0:T(8,128)}, u32[]{:S(2)}) %copy-start.5) | copy-done | bytes 131096
  6.3 0.0 copy-start.6
  6.3 0.9 %copy-done.6 = f32[2,128,128]{2,1,0:T(8,128)S(1)} copy-done((f32[2,128,128]{2,1,0:T(8,128)S(1)}, f32[2,128,128]{2,1,0:T(8,128)}, u32[]{:S(2)}) %copy-start.6) | copy-done | bytes 131096
  7.2 0.0 copy-start.7
  7.2 0.9 %copy-done.7 = f32[256,128]{1,0:T(8,128)S(1)} copy-done((f32[256,128]{1,0:T(8,128)S(1)}, f32[256,128]{1,0:T(8,128)}, u32[]{:S(2)}) %copy-start.7) | copy-done | bytes 131096
  8.1 0.0 copy-start.8
  8.1 0.8 copy-done.8
  8.8 74.1 %shard_map.104 = (f32[16,32,128]{2,1,0:T(8,128)S(1)}, f32[16,32,128]{2,1,0:T(8,128)S(1)}) custom-call(f32[16,32,128]{2,1,0:T(8,128)S(1)} %copy-done, f32[16,32,128]{2,1,0:T(8,128)S(1)} %copy-done.1, f32[8,8,128]{2,1,0:T(8,128)S(1)} %copy-done.8, f32[256,256]{1,0:T(8,128)S(1)} %copy-done.3, f32[256,256]{1,0:T(8,128)S(1)} %copy-done.2, ...), custom_call_target="tpu_custom_call" | custom-call | tf_op jit(solution)/shard_map/pallas_call | solution.py:671
  82.9 0.7 copy.13
  83.6 0.7 copy.14
Async XLA Ops:
  0.6 1.0 %copy-start = (f32[16,32,128]{2,1,0:T(8,128)S(1)}, f32[16,32,128]{2,1,0:T(8,128)}, u32[]{:S(2)}) copy-start(f32[16,32,128]{2,1,0:T(8,128)} %b_ref.1) | copy-start | bytes 786436
  1.6 0.9 %copy-start.1 = (f32[16,32,128]{2,1,0:T(8,128)S(1)}, f32[16,32,128]{2,1,0:T(8,128)}, u32[]{:S(2)}) copy-start(f32[16,32,128]{2,1,0:T(8,128)} %c_ref.1) | copy-start | bytes 786436
  2.5 0.9 %copy-start.2 = (f32[256,256]{1,0:T(8,128)S(1)}, f32[256,256]{1,0:T(8,128)}, u32[]{:S(2)}) copy-start(f32[256,256]{1,0:T(8,128)} %constant.16.clone.rest_2_) | copy-start | bytes 786436
  3.5 0.9 %copy-start.3 = (f32[256,256]{1,0:T(8,128)S(1)}, f32[256,256]{1,0:T(8,128)}, u32[]{:S(2)}) copy-start(f32[256,256]{1,0:T(8,128)} %constant.15.clone.rest_1_) | copy-start | bytes 786436
  4.4 0.9 %copy-start.4 = (f32[2,10,10,128]{3,2,1,0:T(8,128)S(1)}, f32[2,10,10,128]{3,2,1,0:T(8,128)}, u32[]{:S(2)}) copy-start(f32[2,10,10,128]{3,2,1,0:T(8,128)} %constant.19.clone.rest_5_) | copy-start | bytes 307204
  5.3 0.9 %copy-start.5 = (f32[128,256]{1,0:T(8,128)S(1)}, f32[128,256]{1,0:T(8,128)}, u32[]{:S(2)}) copy-start(f32[128,256]{1,0:T(8,128)} %constant.20.clone.rest_6_) | copy-start | bytes 393220
  6.3 0.9 %copy-start.6 = (f32[2,128,128]{2,1,0:T(8,128)S(1)}, f32[2,128,128]{2,1,0:T(8,128)}, u32[]{:S(2)}) copy-start(f32[2,128,128]{2,1,0:T(8,128)} %constant.18.clone.rest_4_) | copy-start | bytes 393220
  7.2 0.9 %copy-start.7 = (f32[256,128]{1,0:T(8,128)S(1)}, f32[256,128]{1,0:T(8,128)}, u32[]{:S(2)}) copy-start(f32[256,128]{1,0:T(8,128)} %constant.17.clone.rest_3_) | copy-start | bytes 393220
  8.1 0.8 copy-start.8

commit v3 on v2

--- a/solution.py
+++ b/solution.py
@@ -102,14 +102,14 @@
         self.corner = 4 * n
         self.z_part = {1: 4 * n + 4, -1: 4 * n + 7 + self.own_z}
         self.total = 4 * n + 10 + 2 * self.own_z
-        self.slot, at, height = {}, 0, 0
+        self.slot, at, height = {}, 0, [0, 0]
         for o in NEAR:
             _, count, tall = self.part(o)
             self.slot[o] = at
             at += count
-            height += count * tall
+            height[tall < 8] += count * tall
         self.received = at
-        self.vectors = height // 8
+        self.vectors = [h // 8 for h in height]
 
     def part(self, o):
         n = self.n
@@ -127,7 +127,6 @@
 
 IN = Halo(SIDE, 7, 6, 0, 1)
 OUT = Halo(BOX, 8, 9, 1, 0)
-RED = (8, 4, 16)
 
 
 def make_kernel(sizes, z_run):
@@ -139,25 +138,22 @@
         tables, rest = rest[:7], rest[7:]
         (sol_ref, res_ref, b_rows, c_rows, wyz_ref, fwd_ref, bwd_ref, asm_ref, der_ref, inv_ref,
          mean_ref, raw, wc, icb, gs, gr, ug, e, x, sp, ss, sr, us, zs, acc,
-         red_y, red_x, red_z, gsend, grecv, ssend, srecv, rsend, rrecv, load) = rest
+         red_xy, red_z, gsend, grecv, ssend, srecv, rsend, rrecv, load) = rest
         gx, gy, gz = (lax.axis_index(a) for a in AXES)
 
         def near(o):
             return ((gx + o[0] + nx) % nx, (gy + o[1] + ny) % ny, (gz + o[2] + nz) % nz)
 
-        def ring_y(t):
-            return (gx, (gy + t) % ny, gz)
-
-        def ring_x(t):
-            return (gx, gy, ((gz // z_run + t) % runs) * z_run + gz % z_run)
+        def ring_xy(t):
+            to = (gz // z_run + t // ny) % runs
+            return (gx, (gy + t % ny) % ny, to * z_run + gz % z_run)
 
         def ring_z(t):
             to = (gx * z_run + gz % z_run + t) % ring
             return (to // z_run, gy, (gz // z_run) * z_run + to % z_run)
 
         partners = [near(o) for o in NEAR]
-        partners += [ring_y(t) for t in range(1, ny)]
-        partners += [ring_x(t) for t in range(1, runs)]
+        partners += [ring_xy(t) for t in range(1, ny * runs)]
         partners += [ring_z(t) for t in range(1, ring)]
         barrier = pltpu.get_barrier_semaphore()
         for device in partners:
@@ -205,16 +201,6 @@
             ]
             return y_hi, y_lo, x_hi, x_lo, corner
 
-        def store_packed(ref, parts, n):
-            for k in range(4):
-                ref[k * n : (k + 1) * n] = parts[k]
-            for k, corner in enumerate(parts[4]):
-                if k % 2 == 0:
-                    corner = jnp.where(sub < 2, rotate(corner, 2, 0), corner)
-                else:
-                    corner = jnp.where(sub < 2, corner, rotate(corner, 6, 0))
-                ref[4 * n + k, 0:4] = corner[0:4]
-
         def lane_pack(values, up):
             total = None
             for k, value in enumerate(values):
@@ -228,38 +214,65 @@
                 turned = jnp.where(ey == k, rotate(value, sign * 32 * k, 1), turned)
             return turned
 
-        def store_lanes(ref, own, parts, halo):
-            for up, base in ((True, halo.z_part[1]), (False, halo.z_part[-1])):
+        def store_and_send(own, planes, lanes, halo, link):
+            src, dst, send_sem, recv_sem = link
+            n = halo.n
+
+            def send(*kinds):
+                for o in NEAR:
+                    if tuple(map(abs, o)) not in kinds:
+                        continue
+                    at, count, tall = halo.part(o)
+                    to = halo.slot[(-o[0], -o[1], -o[2])]
+                    pltpu.make_async_remote_copy(
+                        src_ref=src.at[pl.ds(at, count), pl.ds(0, tall)],
+                        dst_ref=dst.at[pl.ds(to, count), pl.ds(0, tall)],
+                        send_sem=send_sem,
+                        recv_sem=recv_sem.at[1 if tall < 8 else 0],
+                        device_id=near(o),
+                        device_id_type=MESH,
+                    ).start()
+
+            ends = ((True, halo.z_part[1]), (False, halo.z_part[-1]))
+            for up, base in ends:
+                for k in range(2):
+                    edge = [lanes[2 + k][j] for j in range(n)] + lanes[4][2 * k : 2 * k + 2]
+                    moved = fan(lane_pack(edge, up), 1)
+                    moved = jnp.where(lane // 32 == ey, moved, 0.0)
+                    at = base + halo.own_z + 1 + k
+                    src[at, 0:1] = jnp.sum(moved[0:4], axis=0, keepdims=True)
+                    src[at, 1:2] = jnp.sum(moved[4:8], axis=0, keepdims=True)
+            send((1, 1, 1), (1, 0, 1))
+            for k, corner in enumerate(planes[4]):
+                if k % 2 == 0:
+                    corner = jnp.where(sub < 2, rotate(corner, 2, 0), corner)
+                else:
+                    corner = jnp.where(sub < 2, corner, rotate(corner, 6, 0))
+                src[4 * n + k, 0:4] = corner[0:4]
+            send((1, 1, 0))
+            src[2 * n : 3 * n] = planes[2]
+            src[3 * n : 4 * n] = planes[3]
+            send((1, 0, 0))
+            for up, base in ends:
+                edge = [lanes[side][k] for side in (0, 1) for k in range(n)]
+                src[base + halo.own_z] = lane_pack(edge, up)
+            send((0, 1, 1))
+            for up, base in ends:
                 for k in range(halo.own_z):
-                    ref[base + k] = lane_pack(own[64 * k : 64 * k + 64], up)
-                n, at = halo.n, base + halo.own_z
-                planes = [parts[side][k] for side in (0, 1) for k in range(n)]
-                ref[at] = lane_pack(planes, up)
-                for k in range(2):
-                    planes = [parts[2 + k][j] for j in range(n)] + parts[4][2 * k : 2 * k + 2]
-                    moved = fan(lane_pack(planes, up), 1)
-                    moved = jnp.where(lane // 32 == ey, moved, 0.0)
-                    ref[at + 1 + k, 0:1] = jnp.sum(moved[0:4], axis=0, keepdims=True)
-                    ref[at + 1 + k, 1:2] = jnp.sum(moved[4:8], axis=0, keepdims=True)
-
-        def send(src, dst, halo, send_sem, recv_sem):
-            for o in NEAR:
-                at, count, tall = halo.part(o)
-                to = halo.slot[(-o[0], -o[1], -o[2])]
-                pltpu.make_async_remote_copy(
-                    src_ref=src.at[pl.ds(at, count), pl.ds(0, tall)],
-                    dst_ref=dst.at[pl.ds(to, count), pl.ds(0, tall)],
-                    send_sem=send_sem,
-                    recv_sem=recv_sem,
-                    device_id=near(o),
-                    device_id_type=MESH,
-                ).start()
+                    src[base + k] = lane_pack(own[64 * k : 64 * k + 64], up)
+            send((0, 0, 1))
+            src[0:n] = planes[0]
+            src[n : 2 * n] = planes[1]
+            send((0, 1, 0))
 
         def wait_all(ref, sem):
             pltpu.make_async_copy(ref, ref, sem).wait()
 
-        def wait_halo(ref, halo, sem):
-            wait_all(ref.at[pl.ds(0, halo.vectors)], sem)
+        def wait_halo(ref, halo, sem, far):
+            wait_all(ref.at[pl.ds(0, halo.vectors[far])], sem.at[far])
+
+        def wait_sent(ref, halo, sem):
+            wait_all(ref.at[pl.ds(0, sum(halo.vectors))], sem)
 
         def y_lanes(dst, halo, dz):
             low, high = dst[halo.slot[(0, -1, dz)]], dst[halo.slot[(0, 1, dz)]]
@@ -286,12 +299,13 @@
                 lane < 2, rotate(low, -2 * k, 1), rotate(high, 126 - 2 * k, 1)
             )
 
-        def receive(dst, halo, put):
+        def receive(dst, halo, sem, put):
             n = halo.n
 
             def at(o, k=0):
                 return dst[halo.slot[o] + k]
 
+            wait_halo(dst, halo, sem, 0)
             own_lo = [dst[halo.slot[(0, 0, -1)] + k] for k in range(halo.own_z)]
             own_hi = [dst[halo.slot[(0, 0, 1)] + k] for k in range(halo.own_z)]
             for i in range(n):
@@ -299,14 +313,16 @@
                     k = i * n + j
                     put(1, i, j, unlane(own_lo[k // 64], own_hi[k // 64], k % 64))
             low, high = y_lanes(dst, halo, -1), y_lanes(dst, halo, 1)
-            below = x_lanes(dst, halo, -1, -1), x_lanes(dst, halo, -1, 1)
-            above = x_lanes(dst, halo, 1, -1), x_lanes(dst, halo, 1, 1)
             for k in range(n):
                 put(0, k, n, y_mask * jnp.where(ey >= 2, at((0, -1, 0), k), at((0, 1, 0), k)))
                 put(1, k, n, y_mask * unlane(low, high, k))
                 put(0, n, k, fx_lo * at((-1, 0, 0), k))
+                put(0, n + 1, k, fx_hi * at((1, 0, 0), k))
+            wait_halo(dst, halo, sem, 1)
+            below = x_lanes(dst, halo, -1, -1), x_lanes(dst, halo, -1, 1)
+            above = x_lanes(dst, halo, 1, -1), x_lanes(dst, halo, 1, 1)
+            for k in range(n):
                 put(1, n, k, fx_lo * unlane(*below, k))
-                put(0, n + 1, k, fx_hi * at((1, 0, 0), k))
                 put(1, n + 1, k, fx_hi * unlane(*above, k))
             put(0, n, n, fx_lo * y_mask * xy_corner(dst, halo, -1))
             put(1, n, n, fx_lo * y_mask * unlane(*below, n))
@@ -331,15 +347,14 @@
         def gather_send(it):
             u = raw[it].reshape(8, 8, 8, 128)
             parts = pack(u, IN)
-            store_packed(gs.at[it], parts, SIDE)
-            store_lanes(gs.at[it], [raw[it, k] for k in range(64)], parts, IN)
-            send(gs.at[it], gr.at[it], IN, gsend.at[it], grecv.at[it])
+            link = (gs.at[it], gr.at[it], gsend.at[it], grecv.at[it])
+            store_and_send([raw[it, k] for k in range(64)], parts, parts, IN, link)
 
         def gather_receive(it):
             def put(tile, i, j, value):
                 ug[tile, i, j] = value
 
-            receive(gr.at[it], IN, put)
+            receive(gr.at[it], IN, grecv.at[it], put)
             ug[0, 0:8, 0:8] = raw[it].reshape(8, 8, 8, 128)
             for tile in range(2):
                 u = [ug[tile, i] for i in range(10)]
@@ -429,24 +444,22 @@
             sp[1] = back[:, 128:].reshape(10, 10, 8, 128)
 
         def scatter_send(it):
-            store_packed(ss.at[it], pack(sp[0], OUT), BOX)
             own = [sp[1, k // 10, k % 10] for k in range(100)]
-            store_lanes(ss.at[it], own, pack(sp[1], OUT), OUT)
-            send(ss.at[it], sr.at[it], OUT, ssend.at[it], srecv.at[it])
+            link = (ss.at[it], sr.at[it], ssend.at[it], srecv.at[it])
+            store_and_send(own, pack(sp[0], OUT), pack(sp[1], OUT), OUT, link)
 
         def scatter_receive(it):
+            halves = {}
+
             def put(tile, i, j, value):
-                if tile == 0:
-                    us[i, j] = value
+                if i < 10 and j < 10:
+                    us[i, j] = sp[0, i, j] + value
+                elif (i, j) in halves:
+                    us[i, j] = halves.pop((i, j)) + value
                 else:
-                    us[i, j] = us[i, j] + value
-
-            us[0:10, 0:10] = sp[0]
-            later = []
-            receive(sr.at[it], OUT, lambda t, i, j, v: put(t, i, j, v) if t == 0
-                    else later.append((i, j, v)))
-            for i, j, v in later:
-                put(1, i, j, v)
+                    halves[i, j] = value
+
+            receive(sr.at[it], OUT, srecv.at[it], put)
             u = [us[i] for i in range(12)]
             face_lo, next_lo, face_hi, next_hi = from_x(u, u[10], u[11], 8, 9, 1, 0)
             fold = [u[1] + face_lo, u[2] + next_lo, u[3], u[4], u[5], u[6],
@@ -507,13 +520,21 @@
             raw[it + 1] = total.reshape(64, 8, 128)
             acc[2 * it + 1] = jnp.sum((total * field).reshape(64, 8, 128), axis=0)
 
-        rings = ((red_y, ny, gy, ring_y), (red_x, runs, gz // z_run, ring_x),
-                 (red_z, ring, gx * z_run + gz % z_run, ring_z))
+        def far_first(count, length):
+            return sorted(range(1, count), key=lambda t: -length(t))
+
+        rings = (
+            (red_xy, ny * runs, gz // z_run * ny + gy, ring_xy,
+             far_first(ny * runs, lambda t: min(t // ny, runs - t // ny)
+                       + min(t % ny, ny - t % ny) / 2)),
+            (red_z, ring, gx * z_run + gz % z_run, ring_z,
+             far_first(ring, lambda t: min(t, ring - t))),
+        )
 
         def reduce_start(phase, value):
-            ref, count, me, to = rings[phase]
+            ref, count, me, to, order = rings[phase]
             ref[me, 0:1] = value
-            for t in range(1, count):
+            for t in order:
                 pltpu.make_async_remote_copy(
                     src_ref=ref.at[me, pl.ds(0, 1)],
                     dst_ref=ref.at[me, pl.ds(0, 1)],
@@ -524,13 +545,13 @@
                 ).start()
 
         def reduce_wait(phase):
-            ref, count, _, _ = rings[phase]
+            ref, count = rings[phase][:2]
             if count > 1:
                 wait_all(ref.at[pl.ds(0, count - 1), pl.ds(0, 1)], rrecv.at[phase])
             return jnp.sum(ref[0:count, 0:1], axis=0)
 
         def reduce_end(phase):
-            ref, count, _, _ = rings[phase]
+            ref, count = rings[phase][:2]
             if count > 1:
                 wait_all(ref.at[pl.ds(0, count - 1), pl.ds(0, 1)], rsend.at[phase])
 
@@ -561,11 +582,9 @@
             wc[8 * i : 8 * i + 8] = zs[0, 8 * i : 8 * i + 8] * (wyz_ref[...] * float(WEIGHTS[i]))
 
         def step(it, carry):
-            wait_halo(gr.at[it], IN, grecv.at[it])
             gather_receive(it)
             boxes(it)
             scatter_send(it)
-            wait_halo(sr.at[it], OUT, srecv.at[it])
             scatter_receive(it)
             stiffness(it)
 
@@ -582,10 +601,8 @@
 
         lax.fori_loop(0, 2, step, 0)
         reduce_start(1, reduce_wait(0))
-        reduce_start(2, reduce_wait(1))
-        wait_halo(gr.at[2], IN, grecv.at[2])
         gather_receive(2)
-        sums = reduce_wait(2)
+        sums = reduce_wait(1)
         rho, delta, gamma, eps = (sums[:, k : k + 1] for k in range(4))
         a0 = rho / delta
         rz = a0 * a0 * gamma - rho
@@ -611,10 +628,10 @@
                       preferred_element_type=F32)
         write(out.reshape(64, 8, 128), res_ref)
         for it in range(3):
-            wait_halo(gr.at[it], IN, gsend.at[it])
+            wait_sent(gr.at[it], IN, gsend.at[it])
         for it in range(2):
-            wait_halo(sr.at[it], OUT, ssend.at[it])
-        for phase in range(3):
+            wait_sent(sr.at[it], OUT, ssend.at[it])
+        for phase in range(2):
             reduce_end(phase)
 
     return kernel
@@ -659,11 +676,11 @@
             block(3, 2, 64), block(2, 10, 10),
             block(2, OUT.total), block(2, OUT.received), block(12, 11),
             block(2, 64), block(4),
-            block(sizes[1]), block(sizes[2] // z_run), block(ring),
-            dma((3,)), dma((3,)), dma((2,)), dma((2,)), dma((3,)), dma((3,)), dma((11,)),
+            block(sizes[1] * sizes[2] // z_run), block(ring),
+            dma((3,)), dma((3, 2)), dma((2,)), dma((2, 2)), dma((2,)), dma((2,)), dma((11,)),
         ],
         compiler_params=pltpu.CompilerParams(
-            collective_id=0, has_side_effects=True, vmem_limit_bytes=48 * 1024 * 1024
+            collective_id=0, has_side_effects=True, vmem_limit_bytes=60 * 1024 * 1024
         ),
     )
 

time: 84.7 us -> 76.7 us (0.906)
  local copies, waits for them, and re-layouts: 9.58 us -> 2.42 us
    unnamed x20 -> x4, local copies, waits for them, and re-layouts: 9.58 us -> 2.42 us
where the time goes in v3:
time: 76.7 us; the launch traced here: 76.6 us
  Pallas kernels  73.5 us (96%)
  local copies, waits for them, and re-layouts  2.42 us (3%)
    pallas_call x1, Pallas kernels, shards(): return tuple(call(right_side, coefficient, *tables))  73.5 us
    unnamed x4, local copies, waits for them, and re-layouts  2.42 us

profile of v3, /device:TPU:1, one launch (start us, length us, event | category | flops | bytes accessed | tf_op | source)
XLA Modules:
  0.0 76.6 jit_solution(2628429568249642084)
XLA Ops:
  0.6 73.5 %shard_map.104 = (f32[16,32,128]{2,1,0:T(8,128)}, f32[16,32,128]{2,1,0:T(8,128)}) custom-call(f32[16,32,128]{2,1,0:T(8,128)} %b_ref.1, f32[16,32,128]{2,1,0:T(8,128)} %c_ref.1, f32[8,8,128]{2,1,0:T(8,128)} %constant.14.clone.rest_0_, f32[256,256]{1,0:T(8,128)} %constant.15.clone.rest_1_, f32[256,256]{1,0:T(8,128)} %constant.16.clone.rest_2_, ...), custom_call_target="tpu_custom_call" | custom-call | tf_op jit(solution)/shard_map/pallas_call | solution.py:688
  74.1 0.0 copy-start
  74.1 1.7 %copy.13 = f32[16,32,128]{2,1,0:T(8,128)} copy(f32[16,32,128]{2,1,0:T(8,128)} %get-tuple-element.4) | data formatting | bytes 524288
  75.9 0.0 copy-done
  75.9 0.7 copy.14
Async XLA Ops:
  74.1 1.7 %copy-start = (f32[16,32,128]{2,1,0:T(8,128)S(1)}, f32[16,32,128]{2,1,0:T(8,128)}, u32[]{:S(2)}) copy-start(f32[16,32,128]{2,1,0:T(8,128)} %get-tuple-element.5) | copy-start | bytes 786436

commit v4 on v3

--- a/solution.py
+++ b/solution.py
@@ -137,8 +137,8 @@
     def kernel(b_ref, c_ref, *rest):
         tables, rest = rest[:7], rest[7:]
         (sol_ref, res_ref, b_rows, c_rows, wyz_ref, fwd_ref, bwd_ref, asm_ref, der_ref, inv_ref,
-         mean_ref, raw, wc, icb, gs, gr, ug, e, x, sp, ss, sr, us, zs, acc,
-         red_xy, red_z, gsend, grecv, ssend, srecv, rsend, rrecv, load) = rest
+         mean_ref, raw, wc, icb, gs, gr, ug, e, x, sp, sq, fl, ss, sr, us, zs, acc,
+         red_xy, red_z, gsend, grecv, ssend, srecv, rsend, rrecv, load, fin) = rest
         gx, gy, gz = (lax.axis_index(a) for a in AXES)
 
         def near(o):
@@ -188,18 +188,23 @@
         z_mask = jnp.where(lane < 2, fz_lo, jnp.where(lane >= 126, fz_hi, 0.0))
         x_mask = jnp.where(lower, 1.0, fx_hi)
 
-        def pack(u, halo):
-            y_hi = jnp.where(ey == 3, u[:, halo.hf], rotate(u[:, halo.hs], 7, 1))
-            y_lo = jnp.where(ey == 0, u[:, halo.lf], rotate(u[:, halo.ls], 1, 1))
-            x_hi = jnp.where(lower, rotate(u[halo.hs], 4, 1), u[halo.hf])
-            x_lo = jnp.where(lower, u[halo.lf], rotate(u[halo.ls], 4, 1))
-            corner = [
-                jnp.where(lower, rotate(y_hi[halo.hs], 4, 0), y_hi[halo.hf]),
-                jnp.where(lower, rotate(y_lo[halo.hs], 4, 0), y_lo[halo.hf]),
-                jnp.where(lower, y_hi[halo.lf], rotate(y_hi[halo.ls], 4, 0)),
-                jnp.where(lower, y_lo[halo.lf], rotate(y_lo[halo.ls], 4, 0)),
-            ]
-            return y_hi, y_lo, x_hi, x_lo, corner
+        def y_plane(row, halo, up):
+            if up:
+                return jnp.where(ey == 3, row[halo.hf], rotate(row[halo.hs], 7, 0))
+            return jnp.where(ey == 0, row[halo.lf], rotate(row[halo.ls], 1, 0))
+
+        def x_planes(u, halo):
+            out = []
+            for up in (True, False):
+                rows = (halo.hf, halo.hs) if up else (halo.lf, halo.ls)
+                pairs = [(u[rows[0]][j], u[rows[1]][j]) for j in range(halo.n)]
+                pairs += [tuple(y_plane(u[r], halo, y) for r in rows) for y in (True, False)]
+                out.append([
+                    jnp.where(lower, rotate(back, 4, 0), front) if up
+                    else jnp.where(lower, front, rotate(back, 4, 0))
+                    for front, back in pairs
+                ])
+            return out
 
         def lane_pack(values, up):
             total = None
@@ -214,9 +219,10 @@
                 turned = jnp.where(ey == k, rotate(value, sign * 32 * k, 1), turned)
             return turned
 
-        def store_and_send(own, planes, lanes, halo, link):
+        def sender(halo, link):
             src, dst, send_sem, recv_sem = link
             n = halo.n
+            ends = ((True, halo.z_part[1]), (False, halo.z_part[-1]))
 
             def send(*kinds):
                 for o in NEAR:
@@ -233,37 +239,44 @@
                         device_id_type=MESH,
                     ).start()
 
-            ends = ((True, halo.z_part[1]), (False, halo.z_part[-1]))
-            for up, base in ends:
+            def send_x(planes, lanes):
+                lanes, planes = x_planes(lanes, halo), x_planes(planes, halo)
+                for up, base in ends:
+                    for k in range(2):
+                        moved = fan(lane_pack(lanes[k], up), 1)
+                        moved = jnp.where(lane // 32 == ey, moved, 0.0)
+                        at = base + halo.own_z + 1 + k
+                        src[at, 0:1] = jnp.sum(moved[0:4], axis=0, keepdims=True)
+                        src[at, 1:2] = jnp.sum(moved[4:8], axis=0, keepdims=True)
+                send((1, 1, 1), (1, 0, 1))
+                for k in range(4):
+                    corner = planes[k // 2][n + k % 2]
+                    if k % 2 == 0:
+                        corner = jnp.where(sub < 2, rotate(corner, 2, 0), corner)
+                    else:
+                        corner = jnp.where(sub < 2, corner, rotate(corner, 6, 0))
+                    src[4 * n + k, 0:4] = corner[0:4]
+                send((1, 1, 0))
                 for k in range(2):
-                    edge = [lanes[2 + k][j] for j in range(n)] + lanes[4][2 * k : 2 * k + 2]
-                    moved = fan(lane_pack(edge, up), 1)
-                    moved = jnp.where(lane // 32 == ey, moved, 0.0)
-                    at = base + halo.own_z + 1 + k
-                    src[at, 0:1] = jnp.sum(moved[0:4], axis=0, keepdims=True)
-                    src[at, 1:2] = jnp.sum(moved[4:8], axis=0, keepdims=True)
-            send((1, 1, 1), (1, 0, 1))
-            for k, corner in enumerate(planes[4]):
-                if k % 2 == 0:
-                    corner = jnp.where(sub < 2, rotate(corner, 2, 0), corner)
-                else:
-                    corner = jnp.where(sub < 2, corner, rotate(corner, 6, 0))
-                src[4 * n + k, 0:4] = corner[0:4]
-            send((1, 1, 0))
-            src[2 * n : 3 * n] = planes[2]
-            src[3 * n : 4 * n] = planes[3]
-            send((1, 0, 0))
-            for up, base in ends:
-                edge = [lanes[side][k] for side in (0, 1) for k in range(n)]
-                src[base + halo.own_z] = lane_pack(edge, up)
-            send((0, 1, 1))
-            for up, base in ends:
-                for k in range(halo.own_z):
-                    src[base + k] = lane_pack(own[64 * k : 64 * k + 64], up)
-            send((0, 0, 1))
-            src[0:n] = planes[0]
-            src[n : 2 * n] = planes[1]
-            send((0, 1, 0))
+                    for j in range(n):
+                        src[(2 + k) * n + j] = planes[k][j]
+                send((1, 0, 0))
+
+            def send_rest(planes, lanes, own):
+                for up, base in ends:
+                    edge = [y_plane(lanes[i], halo, y) for y in (True, False) for i in range(n)]
+                    src[base + halo.own_z] = lane_pack(edge, up)
+                send((0, 1, 1))
+                for up, base in ends:
+                    for k in range(halo.own_z):
+                        src[base + k] = lane_pack(own[64 * k : 64 * k + 64], up)
+                send((0, 0, 1))
+                for i in range(n):
+                    src[i] = y_plane(planes[i], halo, True)
+                    src[n + i] = y_plane(planes[i], halo, False)
+                send((0, 1, 0))
+
+            return send_x, send_rest
 
         def wait_all(ref, sem):
             pltpu.make_async_copy(ref, ref, sem).wait()
@@ -344,11 +357,16 @@
             next_hi = jnp.where(ey == 3, rotate(h, 2, 1), rotate(u(ls), 7, 1))
             return face_lo, next_lo, face_hi, next_hi
 
-        def gather_send(it):
-            u = raw[it].reshape(8, 8, 8, 128)
-            parts = pack(u, IN)
-            link = (gs.at[it], gr.at[it], gsend.at[it], grecv.at[it])
-            store_and_send([raw[it, k] for k in range(64)], parts, parts, IN, link)
+        def gather_sender(it):
+            return sender(IN, (gs.at[it], gr.at[it], gsend.at[it], grecv.at[it]))
+
+        def gather_x(it):
+            rows = {i: raw[it, 8 * i : 8 * i + 8] for i in (0, 1, 6, 7)}
+            gather_sender(it)[0](rows, rows)
+
+        def gather_rest(it):
+            rows = [raw[it, 8 * i : 8 * i + 8] for i in range(8)]
+            gather_sender(it)[1](rows, rows, [raw[it, k] for k in range(64)])
 
         def gather_receive(it):
             def put(tile, i, j, value):
@@ -373,7 +391,7 @@
                     e[tile, i, 9:10] = next_hi
                 x[it, tile] = e[tile, 1:9, 1:9].reshape(64, 8, 128)
 
-        def halves(v, even, odd):
+        def to_modes(v):
             plus = [v[a] + v[9 - a] for a in range(5)]
             minus = [v[a] - v[9 - a] for a in range(5)]
             out = []
@@ -385,75 +403,85 @@
                 out.append(total)
             return out
 
-        def unhalves(f):
-            first, last = [], []
-            for a in range(5):
+        def from_modes(f, picks=range(5)):
+            out = {}
+            for a in picks:
                 even = f[0] * float(SINE[a, 0])
                 odd = f[1] * float(SINE[a, 1])
                 for k in range(1, 5):
                     even = even + f[2 * k] * float(SINE[a, 2 * k])
                     odd = odd + f[2 * k + 1] * float(SINE[a, 2 * k + 1])
-                first.append(even + odd)
-                last.append(even - odd)
-            return first + last[::-1]
+                out[a], out[9 - a] = even + odd, even - odd
+            return out
 
         def boxes(it):
-            wide = jnp.concatenate(
-                [e[0].reshape(800, 128), e[1].reshape(800, 128)], axis=1
-            )
-            modes = jnp.dot(wide, fwd_ref[...], precision=lax.Precision.HIGH,
-                            preferred_element_type=F32)
-            sp[0] = modes[:, :128].reshape(10, 10, 8, 128)
-            sp[1] = modes[:, 128:].reshape(10, 10, 8, 128)
-
-            def along_x(j, carry):
+            for half in range(2):
+                js = slice(5 * half, 5 * half + 5)
+                wide = jnp.concatenate(
+                    [e[0, :, js].reshape(400, 128), e[1, :, js].reshape(400, 128)], axis=1
+                )
+                modes = jnp.dot(wide, fwd_ref[...], precision=lax.Precision.HIGH,
+                                preferred_element_type=F32)
                 for tile in range(2):
-                    out = halves([sp[tile, i, j] for i in range(10)], None, None)
+                    part = modes[:, 128 * tile : 128 * tile + 128].reshape(10, 5, 8, 128)
+                    out = to_modes([part[i] for i in range(10)])
                     for i in range(10):
-                        sp[tile, i, j] = out[i]
-                return carry
+                        sp[tile, i, js] = out[i]
 
             def middle(i, total):
                 for tile in range(2):
-                    f = halves([sp[tile, i, j] for j in range(10)], None, None)
+                    f = to_modes([sp[tile, i, j] for j in range(10)])
                     scale = icb[tile]
                     g = [f[j] * (inv_ref[tile, i, j : j + 1] * scale) for j in range(10)]
                     for j in range(10):
                         total = total + f[j] * g[j]
-                    out = unhalves(g)
+                    out = from_modes(g)
                     for j in range(10):
                         sp[tile, i, j] = out[j]
                 return total
 
-            def back_x(j, carry):
-                for tile in range(2):
-                    out = unhalves([sp[tile, i, j] for i in range(10)])
-                    for i in range(10):
-                        sp[tile, i, j] = out[i]
-                return carry
-
-            lax.fori_loop(0, 10, along_x, 0)
-            acc[2 * it] = lax.fori_loop(0, 10, middle, jnp.zeros((8, 128), F32))
-            lax.fori_loop(0, 10, back_x, 0)
-            wide = jnp.concatenate(
-                [sp[0].reshape(800, 128), sp[1].reshape(800, 128)], axis=1
-            )
-            back = jnp.dot(wide, bwd_ref[...], precision=lax.Precision.HIGH,
-                           preferred_element_type=F32)
-            sp[0] = back[:, :128].reshape(10, 10, 8, 128)
-            sp[1] = back[:, 128:].reshape(10, 10, 8, 128)
-
-        def scatter_send(it):
-            own = [sp[1, k // 10, k % 10] for k in range(100)]
-            link = (ss.at[it], sr.at[it], ssend.at[it], srecv.at[it])
-            store_and_send(own, pack(sp[0], OUT), pack(sp[1], OUT), OUT, link)
+            acc[2 * it] = lax.fori_loop(0, 10, middle, jnp.zeros((8, 128), F32), unroll=5)
+            send_x, send_rest = sender(OUT, (ss.at[it], sr.at[it], ssend.at[it], srecv.at[it]))
+
+            def answers(picks, spans):
+                def back_x(j, carry):
+                    for tile in range(2):
+                        out = from_modes([sp[tile, i, j] for i in range(10)], picks)
+                        for i, value in out.items():
+                            sq[tile, i, j] = value
+                    return carry
+
+                lax.fori_loop(0, 10, back_x, 0, unroll=5)
+                wide = jnp.concatenate(
+                    [
+                        jnp.concatenate([sq[tile, i0:i1] for i0, i1 in spans]).reshape(-1, 128)
+                        for tile in range(2)
+                    ],
+                    axis=1,
+                )
+                back = jnp.dot(wide, bwd_ref[...], precision=lax.Precision.HIGH,
+                               preferred_element_type=F32)
+                at = 0
+                for i0, i1 in spans:
+                    rows = back[80 * at : 80 * (at + i1 - i0)]
+                    for tile in range(2):
+                        sq[tile, i0:i1] = rows[:, 128 * tile : 128 * tile + 128].reshape(
+                            i1 - i0, 10, 8, 128
+                        )
+                    at += i1 - i0
+
+            answers((0, 1), ((0, 2), (8, 10)))
+            send_x({i: sq[0, i] for i in (0, 1, 8, 9)}, {i: sq[1, i] for i in (0, 1, 8, 9)})
+            answers((2, 3, 4), ((2, 8),))
+            own = [sq[1, k // 10, k % 10] for k in range(100)]
+            send_rest([sq[0, i] for i in range(10)], [sq[1, i] for i in range(10)], own)
 
         def scatter_receive(it):
             halves = {}
 
             def put(tile, i, j, value):
                 if i < 10 and j < 10:
-                    us[i, j] = sp[0, i, j] + value
+                    us[i, j] = sq[0, i, j] + value
                 elif (i, j) in halves:
                     us[i, j] = halves.pop((i, j)) + value
                 else:
@@ -476,49 +504,67 @@
                 zs[it, 8 * i + 6 : 8 * i + 7] = (w[7:8] + next_hi) * last
                 zs[it, 8 * i + 7 : 8 * i + 8] = (w[8:9] + face_hi) * last
 
-        def derive(v, matrix):
+        def derive(v, matrix, picks=range(4)):
             plus = [v[k] + v[7 - k] for k in range(4)]
             minus = [v[k] - v[7 - k] for k in range(4)]
-            first, last = [], []
-            for a in range(4):
+            out = {}
+            for a in picks:
                 even = odd = None
                 for k in range(4):
                     p = plus[k] * float(0.5 * (matrix[a, k] + matrix[a, 7 - k]))
                     m = minus[k] * float(0.5 * (matrix[a, k] - matrix[a, 7 - k]))
                     even = p if even is None else even + p
                     odd = m if odd is None else odd + m
-                first.append(even + odd)
-                last.append(odd - even)
-            return first + last[::-1]
-
-        def stiffness(it):
+                out[a], out[7 - a] = even + odd, odd - even
+            return out
+
+        def fluxes(it):
+            def over_x(j, total):
+                grad = derive([zs[it, 8 * i + j] for i in range(8)], DERIV)
+                for i in range(8):
+                    flux = grad[i] * wc[8 * i + j]
+                    total = total + flux * grad[i]
+                    fl[0, 8 * i + j] = flux
+                return total
+
+            def over_y(i, total):
+                grad = derive([zs[it, 8 * i + j] for j in range(8)], DERIV)
+                for j in range(8):
+                    flux = grad[j] * wc[8 * i + j]
+                    total = total + flux * grad[j]
+                    fl[1, 8 * i + j] = flux
+                return total
+
+            grad = jnp.dot(zs[it].reshape(512, 128), der_ref[0], precision=lax.Precision.HIGH,
+                           preferred_element_type=F32).reshape(64, 8, 128)
+            flux = grad * wc[...]
+            fl[2] = flux
+            total = jnp.sum(flux * grad, axis=0)
+            total = lax.fori_loop(0, 8, over_x, total, unroll=8)
+            acc[2 * it + 1] = lax.fori_loop(0, 8, over_y, total, unroll=8)
+
+        def divergence(it, picks, spans):
+            along_z = jnp.dot(
+                jnp.concatenate([fl[2, 8 * i0 : 8 * i1] for i0, i1 in spans]).reshape(-1, 128),
+                der_ref[1], precision=lax.Precision.HIGH, preferred_element_type=F32,
+            ).reshape(-1, 8, 128)
+            at = 0
+            for i0, i1 in spans:
+                raw[it + 1, 8 * i0 : 8 * i1] = along_z[at : at + 8 * (i1 - i0)]
+                at += 8 * (i1 - i0)
+
             def over_x(j, carry):
-                grad = derive([zs[it, 8 * i + j] for i in range(8)], DERIV)
-                flux = [grad[i] * wc[8 * i + j] for i in range(8)]
-                out = derive(flux, DERIV.T)
-                for i in range(8):
-                    raw[it + 1, 8 * i + j] = out[i]
+                out = derive([fl[0, 8 * i + j] for i in range(8)], DERIV.T, picks)
+                for i, value in out.items():
+                    raw[it + 1, 8 * i + j] = raw[it + 1, 8 * i + j] + value
                 return carry
 
-            def over_y(i, carry):
-                grad = derive([zs[it, 8 * i + j] for j in range(8)], DERIV)
-                flux = [grad[j] * wc[8 * i + j] for j in range(8)]
-                out = derive(flux, DERIV.T)
-                for j in range(8):
-                    raw[it + 1, 8 * i + j] = raw[it + 1, 8 * i + j] + out[j]
-                return carry
-
-            lax.fori_loop(0, 8, over_x, 0)
-            lax.fori_loop(0, 8, over_y, 0)
-            field = zs[it].reshape(512, 128)
-            grad = jnp.dot(field, der_ref[0], precision=lax.Precision.HIGH,
-                           preferred_element_type=F32)
-            flux = grad * wc[...].reshape(512, 128)
-            out = jnp.dot(flux, der_ref[1], precision=lax.Precision.HIGH,
-                          preferred_element_type=F32)
-            total = raw[it + 1].reshape(512, 128) + out
-            raw[it + 1] = total.reshape(64, 8, 128)
-            acc[2 * it + 1] = jnp.sum((total * field).reshape(64, 8, 128), axis=0)
+            lax.fori_loop(0, 8, over_x, 0, unroll=8)
+            for i0, i1 in spans:
+                for i in range(i0, i1):
+                    out = derive([fl[1, 8 * i + j] for j in range(8)], DERIV.T)
+                    for j in range(8):
+                        raw[it + 1, 8 * i + j] = raw[it + 1, 8 * i + j] + out[j]
 
         def far_first(count, length):
             return sorted(range(1, count), key=lambda t: -length(t))
@@ -570,7 +616,8 @@
         loads[1].wait()
         relaid(b_rows, put_b)
         pl.semaphore_wait(barrier, len(partners))
-        gather_send(0)
+        gather_x(0)
+        gather_rest(0)
         for copy in loads[2:]:
             copy.wait()
         relaid(c_rows, put_c)
@@ -584,9 +631,8 @@
         def step(it, carry):
             gather_receive(it)
             boxes(it)
-            scatter_send(it)
             scatter_receive(it)
-            stiffness(it)
+            fluxes(it)
 
             @pl.when(it == 1)
             def _():
@@ -596,12 +642,31 @@
                     local = jnp.where(lane[0:1] == k, total, local)
                 reduce_start(0, local)
 
-            gather_send(it + 1)
+            divergence(it, (0, 1), ((0, 2), (6, 8)))
+            gather_x(it + 1)
+            divergence(it, (2, 3), ((2, 6),))
+            gather_rest(it + 1)
             return carry
 
         lax.fori_loop(0, 2, step, 0)
         reduce_start(1, reduce_wait(0))
         gather_receive(2)
+        def placed(k, values):
+            for m in range(64):
+                for ex in range(2):
+                    fin[k, 8 * ex + m // 8, pl.ds(m % 8, 4, stride=8), :] = values[
+                        m, 4 * ex : 4 * ex + 4
+                    ]
+
+        placed(0, zs[0])
+        placed(1, zs[1])
+        for it in range(3):
+            wide = jnp.concatenate(
+                [x[it, 0].reshape(512, 128), x[it, 1].reshape(512, 128)], axis=1
+            )
+            out = jnp.dot(wide, asm_ref[...], precision=lax.Precision.HIGH,
+                          preferred_element_type=F32)
+            placed(2 + it, out.reshape(64, 8, 128))
         sums = reduce_wait(1)
         rho, delta, gamma, eps = (sums[:, k : k + 1] for k in range(4))
         a0 = rho / delta
@@ -611,22 +676,16 @@
         a1 = rz / curve
         first = a0 + a1 * up
         second = a1 * a0
-
-        def write(values, ref):
-            for k in range(64):
-                for ex in range(2):
-                    ref[8 * ex + k // 8, pl.ds(k % 8, 4, stride=8), :] = values[
-                        k, 4 * ex : 4 * ex + 4
-                    ]
-
-        write(zs[0] * first - zs[1] * second, sol_ref)
-        mixed = x[0] - x[1] * first + x[2] * second
-        wide = jnp.concatenate(
-            [mixed[0].reshape(512, 128), mixed[1].reshape(512, 128)], axis=1
-        )
-        out = jnp.dot(wide, asm_ref[...], precision=lax.Precision.HIGH,
-                      preferred_element_type=F32)
-        write(out.reshape(64, 8, 128), res_ref)
+        stores = [
+            pltpu.make_async_copy(fin.at[k], ref, load.at[k])
+            for k, ref in ((0, sol_ref), (2, res_ref))
+        ]
+        fin[0] = fin[0] * first - fin[1] * second
+        stores[0].start()
+        fin[2] = fin[2] - fin[3] * first + fin[4] * second
+        stores[1].start()
+        for copy in stores:
+            copy.wait()
         for it in range(3):
             wait_sent(gr.at[it], IN, gsend.at[it])
         for it in range(2):
@@ -657,7 +716,7 @@
         jnp.asarray(t, F32)
         for t in (wyz, forward, forward.T, assemble, np.stack([der.T, der]), inverse, mean)
     ]
-    vmem = pl.BlockSpec(memory_space=pltpu.VMEM)
+    hbm = pl.BlockSpec(memory_space=pltpu.HBM)
     dma = pltpu.SemaphoreType.DMA
 
     def block(*shape):
@@ -666,26 +725,44 @@
     call = pl.pallas_call(
         make_kernel(sizes, z_run),
         out_shape=[jax.ShapeDtypeStruct((16, 32, 128), F32)] * 2,
-        in_specs=[pl.BlockSpec(memory_space=pltpu.HBM)] * 9,
-        out_specs=[vmem] * 2,
+        in_specs=[hbm] * 9,
+        out_specs=[hbm] * 2,
         scratch_shapes=[
             pltpu.VMEM((8, 64, 128), F32), pltpu.VMEM((8, 64, 128), F32),
             *[pltpu.VMEM(t.shape, F32) for t in tables],
             block(3, 64), block(64), block(2),
             block(3, IN.total), block(3, IN.received), block(2, 10, 9), block(2, 10, 10),
-            block(3, 2, 64), block(2, 10, 10),
+            block(3, 2, 64), block(2, 10, 10), block(2, 10, 10), block(3, 64),
             block(2, OUT.total), block(2, OUT.received), block(12, 11),
             block(2, 64), block(4),
             block(sizes[1] * sizes[2] // z_run), block(ring),
-            dma((3,)), dma((3, 2)), dma((2,)), dma((2, 2)), dma((2,)), dma((2,)), dma((11,)),
+            dma((3,)), dma((3, 2)), dma((2,)), dma((2, 2)), dma((2,)), dma((2,)), dma((11,)), pltpu.VMEM((5, 16, 32, 128), F32),
         ],
         compiler_params=pltpu.CompilerParams(
             collective_id=0, has_side_effects=True, vmem_limit_bytes=60 * 1024 * 1024
         ),
     )
 
+    def hand_over(first, second, first_out, second_out, sems):
+        copies = [
+            pltpu.make_async_copy(source, target, sems.at[k])
+            for k, (source, target) in enumerate(((first, first_out), (second, second_out)))
+        ]
+        for copy in copies:
+            copy.start()
+        for copy in copies:
+            copy.wait()
+
+    results = pl.pallas_call(
+        hand_over,
+        out_shape=[jax.ShapeDtypeStruct((16, 32, 128), F32)] * 2,
+        in_specs=[pl.BlockSpec(memory_space=pltpu.VMEM)] * 2,
+        out_specs=[hbm] * 2,
+        scratch_shapes=[dma((2,))],
+    )
+
     def shards(right_side, coefficient):
-        return tuple(call(right_side, coefficient, *tables))
+        return tuple(results(*call(right_side, coefficient, *tables)))
 
     spec = P(*AXES)
     return jax.shard_map(

time: 76.7 us -> 73.2 us (0.954)
  local copies, waits for them, and re-layouts: 2.42 us -> 0 us
  Pallas kernels: 73.5 us -> 72.4 us
    unnamed x4 -> x0, local copies, waits for them, and re-layouts: 2.42 us -> none
    pallas_call x1 -> x2, Pallas kernels: 73.5 us -> 72.4 us  [shards(): return tuple(results(*call(right_side, coefficient, *tables)))]
where the time goes in v4:
time: 73.2 us; the launch traced here: 73 us
  Pallas kernels  72.4 us (99%)
    pallas_call x2, Pallas kernels, shards(): return tuple(results(*call(right_side, coefficient, *tables)))  72.4 us

profile of v4, /device:TPU:1, one launch (start us, length us, event | category | flops | bytes accessed | tf_op | source)
XLA Modules:
  0.0 73.0 jit_solution(6303500591331243509)
XLA Ops:
  0.6 70.5 %shard_map.104 = (f32[16,32,128]{2,1,0:T(8,128)}, f32[16,32,128]{2,1,0:T(8,128)}) custom-call(f32[16,32,128]{2,1,0:T(8,128)} %b_ref.1, f32[16,32,128]{2,1,0:T(8,128)} %c_ref.1, f32[8,8,128]{2,1,0:T(8,128)} %constant.14.clone.rest_0_, f32[256,256]{1,0:T(8,128)} %constant.15.clone.rest_1_, f32[256,256]{1,0:T(8,128)} %constant.16.clone.rest_2_, ...), custom_call_target="tpu_custom_call" | custom-call | tf_op jit(solution)/shard_map/pallas_call | solution.py:765
  71.2 1.8 %shard_map.105 = (f32[16,32,128]{2,1,0:T(8,128)}, f32[16,32,128]{2,1,0:T(8,128)}) custom-call(f32[16,32,128]{2,1,0:T(8,128)} %get-tuple-element.4.first, f32[16,32,128]{2,1,0:T(8,128)} %get-tuple-element.5.second), custom_call_target="tpu_custom_call" | custom-call | tf_op jit(solution)/shard_map/pallas_call | solution.py:765

commit v5 on v4

--- a/solution.py
+++ b/solution.py
@@ -312,7 +312,7 @@
                 lane < 2, rotate(low, -2 * k, 1), rotate(high, 126 - 2 * k, 1)
             )
 
-        def receive(dst, halo, sem, put):
+        def receive_near(dst, halo, sem, put):
             n = halo.n
 
             def at(o, k=0):
@@ -331,6 +331,8 @@
                 put(1, k, n, y_mask * unlane(low, high, k))
                 put(0, n, k, fx_lo * at((-1, 0, 0), k))
                 put(0, n + 1, k, fx_hi * at((1, 0, 0), k))
+        def receive_far(dst, halo, sem, put):
+            n = halo.n
             wait_halo(dst, halo, sem, 1)
             below = x_lanes(dst, halo, -1, -1), x_lanes(dst, halo, -1, 1)
             above = x_lanes(dst, halo, 1, -1), x_lanes(dst, halo, 1, 1)
@@ -368,38 +370,47 @@
             rows = [raw[it, 8 * i : 8 * i + 8] for i in range(8)]
             gather_sender(it)[1](rows, rows, [raw[it, k] for k in range(64)])
 
-        def gather_receive(it):
-            def put(tile, i, j, value):
-                ug[tile, i, j] = value
-
-            receive(gr.at[it], IN, grecv.at[it], put)
+        def spread_rows(tile, rows):
+            for i, w in rows.items():
+                face_lo, next_lo, face_hi, next_hi = from_y(
+                    lambda j: w[j : j + 1], w[8:9], 7, 6, 0, 1
+                )
+                e[tile, i, 0:1] = next_lo
+                e[tile, i, 1:2] = w[0:1] + face_lo
+                e[tile, i, 2:8] = w[1:7]
+                e[tile, i, 8:9] = w[7:8] + face_hi
+                e[tile, i, 9:10] = next_hi
+
+        def put_gathered(tile, i, j, value):
+            ug[tile, i, j] = value
+
+        def gather_near(it):
+            receive_near(gr.at[it], IN, grecv.at[it], put_gathered)
             ug[0, 0:8, 0:8] = raw[it].reshape(8, 8, 8, 128)
+            for tile in range(2):
+                spread_rows(tile, {i + 1: ug[tile, i] for i in range(1, 7)})
+
+        def gather_far(it):
+            receive_far(gr.at[it], IN, grecv.at[it], put_gathered)
             for tile in range(2):
                 u = [ug[tile, i] for i in range(10)]
                 face_lo, next_lo, face_hi, next_hi = from_x(u, u[8], u[9], 7, 6, 0, 1)
-                wide = [next_lo, u[0] + face_lo] + u[1:7]
-                wide += [(u[7] + face_hi) * x_mask, next_hi]
-                for i in range(10):
-                    w = wide[i]
-                    face_lo, next_lo, face_hi, next_hi = from_y(
-                        lambda j: w[j : j + 1], w[8:9], 7, 6, 0, 1
-                    )
-                    e[tile, i, 0:1] = next_lo
-                    e[tile, i, 1:2] = w[0:1] + face_lo
-                    e[tile, i, 2:8] = w[1:7]
-                    e[tile, i, 8:9] = w[7:8] + face_hi
-                    e[tile, i, 9:10] = next_hi
+                spread_rows(tile, {0: next_lo, 1: u[0] + face_lo,
+                                   8: (u[7] + face_hi) * x_mask, 9: next_hi})
+
+        def gather_keep(it):
+            for tile in range(2):
                 x[it, tile] = e[tile, 1:9, 1:9].reshape(64, 8, 128)
 
-        def to_modes(v):
-            plus = [v[a] + v[9 - a] for a in range(5)]
-            minus = [v[a] - v[9 - a] for a in range(5)]
+        def to_modes(v, picks=range(5)):
+            plus = {a: v[a] + v[9 - a] for a in picks}
+            minus = {a: v[a] - v[9 - a] for a in picks}
             out = []
             for k in range(10):
-                part = plus if k % 2 == 0 else minus
-                total = part[0] * float(SINE[0, k])
-                for a in range(1, 5):
-                    total = total + part[a] * float(SINE[a, k])
+                total = None
+                for a in picks:
+                    term = (plus if k % 2 == 0 else minus)[a] * float(SINE[a, k])
+                    total = term if total is None else total + term
                 out.append(total)
             return out
 
@@ -414,86 +425,109 @@
                 out[a], out[9 - a] = even + odd, even - odd
             return out
 
+        def joined_rows(ref, spans):
+            return jnp.concatenate(
+                [
+                    jnp.concatenate([ref[tile, i0:i1] for i0, i1 in spans]).reshape(-1, 128)
+                    for tile in range(2)
+                ],
+                axis=1,
+            )
+
+        def store_rows(ref, spans, values):
+            at = 0
+            for i0, i1 in spans:
+                rows = values[80 * at : 80 * (at + i1 - i0)]
+                for tile in range(2):
+                    ref[tile, i0:i1] = rows[:, 128 * tile : 128 * tile + 128].reshape(
+                        i1 - i0, 10, 8, 128
+                    )
+                at += i1 - i0
+
+        def row_modes(spans):
+            modes = jnp.dot(joined_rows(e, spans), fwd_ref[...], precision=lax.Precision.HIGH,
+                            preferred_element_type=F32)
+            store_rows(sq, spans, modes)
+            for i0, i1 in spans:
+                def over_y(i, carry):
+                    for tile in range(2):
+                        out = to_modes([sq[tile, i, j] for j in range(10)])
+                        for j in range(10):
+                            sq[tile, i, j] = out[j]
+                    return carry
+
+                lax.fori_loop(i0, i1, over_y, 0, unroll=i1 - i0)
+
+        def near_modes():
+            row_modes(((2, 8),))
+
+            def over_x(j, carry):
+                for tile in range(2):
+                    out = to_modes({i: sq[tile, i, j] for i in range(2, 8)}, (2, 3, 4))
+                    for i in range(10):
+                        sp[tile, i, j] = out[i]
+                return carry
+
+            lax.fori_loop(0, 10, over_x, 0, unroll=5)
+
         def boxes(it):
-            for half in range(2):
-                js = slice(5 * half, 5 * half + 5)
-                wide = jnp.concatenate(
-                    [e[0, :, js].reshape(400, 128), e[1, :, js].reshape(400, 128)], axis=1
-                )
-                modes = jnp.dot(wide, fwd_ref[...], precision=lax.Precision.HIGH,
-                                preferred_element_type=F32)
+            row_modes(((0, 2), (8, 10)))
+
+            def middle(j, total):
                 for tile in range(2):
-                    part = modes[:, 128 * tile : 128 * tile + 128].reshape(10, 5, 8, 128)
-                    out = to_modes([part[i] for i in range(10)])
+                    f = to_modes({i: sq[tile, i, j] for i in (0, 1, 8, 9)}, (0, 1))
+                    f = [f[i] + sp[tile, i, j] for i in range(10)]
+                    scale = icb[tile]
+                    g = [f[i] * (inv_ref[tile, j, i : i + 1] * scale) for i in range(10)]
                     for i in range(10):
-                        sp[tile, i, js] = out[i]
-
-            def middle(i, total):
-                for tile in range(2):
-                    f = to_modes([sp[tile, i, j] for j in range(10)])
-                    scale = icb[tile]
-                    g = [f[j] * (inv_ref[tile, i, j : j + 1] * scale) for j in range(10)]
-                    for j in range(10):
-                        total = total + f[j] * g[j]
-                    out = from_modes(g)
-                    for j in range(10):
-                        sp[tile, i, j] = out[j]
+                        total = total + f[i] * g[i]
+                        sp[tile, i, j] = g[i]
+                    for i, value in from_modes(g, (0, 1)).items():
+                        sq[tile, i, j] = value
                 return total
 
             acc[2 * it] = lax.fori_loop(0, 10, middle, jnp.zeros((8, 128), F32), unroll=5)
             send_x, send_rest = sender(OUT, (ss.at[it], sr.at[it], ssend.at[it], srecv.at[it]))
 
-            def answers(picks, spans):
-                def back_x(j, carry):
-                    for tile in range(2):
-                        out = from_modes([sp[tile, i, j] for i in range(10)], picks)
-                        for i, value in out.items():
-                            sq[tile, i, j] = value
-                    return carry
-
-                lax.fori_loop(0, 10, back_x, 0, unroll=5)
-                wide = jnp.concatenate(
-                    [
-                        jnp.concatenate([sq[tile, i0:i1] for i0, i1 in spans]).reshape(-1, 128)
-                        for tile in range(2)
-                    ],
-                    axis=1,
-                )
-                back = jnp.dot(wide, bwd_ref[...], precision=lax.Precision.HIGH,
-                               preferred_element_type=F32)
-                at = 0
+            def answers(spans):
                 for i0, i1 in spans:
-                    rows = back[80 * at : 80 * (at + i1 - i0)]
-                    for tile in range(2):
-                        sq[tile, i0:i1] = rows[:, 128 * tile : 128 * tile + 128].reshape(
-                            i1 - i0, 10, 8, 128
-                        )
-                    at += i1 - i0
-
-            answers((0, 1), ((0, 2), (8, 10)))
+                    def back_y(i, carry):
+                        for tile in range(2):
+                            out = from_modes([sq[tile, i, j] for j in range(10)])
+                            for j, value in out.items():
+                                sq[tile, i, j] = value
+                        return carry
+
+                    lax.fori_loop(i0, i1, back_y, 0, unroll=i1 - i0)
+                back = jnp.dot(joined_rows(sq, spans), bwd_ref[...],
+                               precision=lax.Precision.HIGH, preferred_element_type=F32)
+                store_rows(sq, spans, back)
+
+            answers(((0, 2), (8, 10)))
             send_x({i: sq[0, i] for i in (0, 1, 8, 9)}, {i: sq[1, i] for i in (0, 1, 8, 9)})
-            answers((2, 3, 4), ((2, 8),))
+
+            def back_x(j, carry):
+                for tile in range(2):
+                    out = from_modes([sp[tile, i, j] for i in range(10)], (2, 3, 4))
+                    for i, value in out.items():
+                        sq[tile, i, j] = value
+                return carry
+
+            lax.fori_loop(0, 10, back_x, 0, unroll=5)
+            answers(((2, 8),))
             own = [sq[1, k // 10, k % 10] for k in range(100)]
             send_rest([sq[0, i] for i in range(10)], [sq[1, i] for i in range(10)], own)
 
-        def scatter_receive(it):
-            halves = {}
-
-            def put(tile, i, j, value):
-                if i < 10 and j < 10:
-                    us[i, j] = sq[0, i, j] + value
-                elif (i, j) in halves:
-                    us[i, j] = halves.pop((i, j)) + value
-                else:
-                    halves[i, j] = value
-
-            receive(sr.at[it], OUT, srecv.at[it], put)
-            u = [us[i] for i in range(12)]
-            face_lo, next_lo, face_hi, next_hi = from_x(u, u[10], u[11], 8, 9, 1, 0)
-            fold = [u[1] + face_lo, u[2] + next_lo, u[3], u[4], u[5], u[6],
-                    u[7] + next_hi, (u[8] + face_hi) * x_mask]
-            for i in range(8):
-                w = fold[i]
+        def put_scattered(tile, i, j, value):
+            if i < 10 and j < 10:
+                us[i, j] = sq[0, i, j] + value
+            elif tile == 0:
+                us[i, j] = value
+            else:
+                us[i, j] = us[i, j] + value
+
+        def fold_rows(it, rows):
+            for i, w in rows.items():
                 last = x_mask if i == 7 else 1.0
                 face_lo, next_lo, face_hi, next_hi = from_y(
                     lambda j: w[j : j + 1], w[10:11], 8, 9, 1, 0
@@ -503,6 +537,17 @@
                 zs[it, 8 * i + 2 : 8 * i + 6] = w[3:7] * last
                 zs[it, 8 * i + 6 : 8 * i + 7] = (w[7:8] + next_hi) * last
                 zs[it, 8 * i + 7 : 8 * i + 8] = (w[8:9] + face_hi) * last
+
+        def scatter_near(it):
+            receive_near(sr.at[it], OUT, srecv.at[it], put_scattered)
+            fold_rows(it, {i: us[i + 1] for i in range(2, 6)})
+
+        def scatter_far(it):
+            receive_far(sr.at[it], OUT, srecv.at[it], put_scattered)
+            u = [us[i] for i in range(12)]
+            face_lo, next_lo, face_hi, next_hi = from_x(u, u[10], u[11], 8, 9, 1, 0)
+            fold_rows(it, {0: u[1] + face_lo, 1: u[2] + next_lo, 6: u[7] + next_hi,
+                           7: (u[8] + face_hi) * x_mask})
 
         def derive(v, matrix, picks=range(4)):
             plus = [v[k] + v[7 - k] for k in range(4)]
@@ -518,7 +563,28 @@
                 out[a], out[7 - a] = even + odd, odd - even
             return out
 
-        def fluxes(it):
+        def fluxes_in_planes(it, spans):
+            def joined(ref):
+                return jnp.concatenate([ref[8 * i0 : 8 * i1] for i0, i1 in spans])
+
+            grad = jnp.dot(joined(zs.at[it]).reshape(-1, 128), der_ref[0],
+                           precision=lax.Precision.HIGH,
+                           preferred_element_type=F32).reshape(-1, 8, 128)
+            flux = grad * joined(wc)
+            total = jnp.sum(flux * grad, axis=0)
+            at = 0
+            for i0, i1 in spans:
+                fl[2, 8 * i0 : 8 * i1] = flux[at : at + 8 * (i1 - i0)]
+                at += 8 * (i1 - i0)
+                for i in range(i0, i1):
+                    along = derive([zs[it, 8 * i + j] for j in range(8)], DERIV)
+                    for j in range(8):
+                        part = along[j] * wc[8 * i + j]
+                        total = total + part * along[j]
+                        fl[1, 8 * i + j] = part
+            return total
+
+        def fluxes_across(it, total):
             def over_x(j, total):
                 grad = derive([zs[it, 8 * i + j] for i in range(8)], DERIV)
                 for i in range(8):
@@ -527,21 +593,7 @@
                     fl[0, 8 * i + j] = flux
                 return total
 
-            def over_y(i, total):
-                grad = derive([zs[it, 8 * i + j] for j in range(8)], DERIV)
-                for j in range(8):
-                    flux = grad[j] * wc[8 * i + j]
-                    total = total + flux * grad[j]
-                    fl[1, 8 * i + j] = flux
-                return total
-
-            grad = jnp.dot(zs[it].reshape(512, 128), der_ref[0], precision=lax.Precision.HIGH,
-                           preferred_element_type=F32).reshape(64, 8, 128)
-            flux = grad * wc[...]
-            fl[2] = flux
-            total = jnp.sum(flux * grad, axis=0)
-            total = lax.fori_loop(0, 8, over_x, total, unroll=8)
-            acc[2 * it + 1] = lax.fori_loop(0, 8, over_y, total, unroll=8)
+            return lax.fori_loop(0, 8, over_x, total, unroll=8)
 
         def divergence(it, picks, spans):
             along_z = jnp.dot(
@@ -629,10 +681,16 @@
             wc[8 * i : 8 * i + 8] = zs[0, 8 * i : 8 * i + 8] * (wyz_ref[...] * float(WEIGHTS[i]))
 
         def step(it, carry):
-            gather_receive(it)
+            gather_near(it)
+            near_modes()
+            gather_far(it)
             boxes(it)
-            scatter_receive(it)
-            fluxes(it)
+            gather_keep(it)
+            scatter_near(it)
+            total = fluxes_in_planes(it, ((2, 6),))
+            scatter_far(it)
+            total = total + fluxes_in_planes(it, ((0, 2), (6, 8)))
+            acc[2 * it + 1] = fluxes_across(it, total)
 
             @pl.when(it == 1)
             def _():
@@ -650,7 +708,9 @@
 
         lax.fori_loop(0, 2, step, 0)
         reduce_start(1, reduce_wait(0))
-        gather_receive(2)
+        gather_near(2)
+        gather_far(2)
+        gather_keep(2)
         def placed(k, values):
             for m in range(64):
                 for ex in range(2):
@@ -743,22 +803,35 @@
         ),
     )
 
-    def hand_over(first, second, first_out, second_out, sems):
-        copies = [
-            pltpu.make_async_copy(source, target, sems.at[k])
-            for k, (source, target) in enumerate(((first, first_out), (second, second_out)))
+    def hand_over(first, second, first_out, second_out, held, sems):
+        pieces = [
+            (source, target, pl.ds(8 * half, 8))
+            for source, target in ((first, first_out), (second, second_out))
+            for half in range(2)
         ]
-        for copy in copies:
+        reads = [
+            pltpu.make_async_copy(source.at[part], held.at[k], sems.at[0, k])
+            for k, (source, _, part) in enumerate(pieces)
+        ]
+        writes = [
+            pltpu.make_async_copy(held.at[k], target.at[part], sems.at[1, k])
+            for k, (_, target, part) in enumerate(pieces)
+        ]
+        for copy in reads:
             copy.start()
-        for copy in copies:
+        for read, write in zip(reads, writes):
+            read.wait()
+            write.start()
+        for copy in writes:
             copy.wait()
 
     results = pl.pallas_call(
         hand_over,
         out_shape=[jax.ShapeDtypeStruct((16, 32, 128), F32)] * 2,
-        in_specs=[pl.BlockSpec(memory_space=pltpu.VMEM)] * 2,
+        in_specs=[hbm] * 2,
         out_specs=[hbm] * 2,
-        scratch_shapes=[dma((2,))],
+        scratch_shapes=[pltpu.VMEM((4, 8, 32, 128), F32), dma((2, 4))],
+        compiler_params=pltpu.CompilerParams(vmem_limit_bytes=60 * 1024 * 1024),
     )
 
     def shards(right_side, coefficient):

time: 73.2 us -> 72.1 us (0.985)
  Pallas kernels: 72.4 us -> 71.3 us
    pallas_call x2, Pallas kernels: 72.4 us -> 71.3 us  [shards(): return tuple(results(*call(right_side, coefficient, *tables)))]
where the time goes in v5:
time: 72.1 us; the launch traced here: 72 us
  Pallas kernels  71.3 us (99%)
    pallas_call x2, Pallas kernels, shards(): return tuple(results(*call(right_side, coefficient, *tables)))  71.3 us

profile of v5, /device:TPU:1, one launch (start us, length us, event | category | flops | bytes accessed | tf_op | source)
XLA Modules:
  0.0 72.0 jit_solution(14038862679394415121)
XLA Ops:
  0.6 69.5 %shard_map.104 = (f32[16,32,128]{2,1,0:T(8,128)}, f32[16,32,128]{2,1,0:T(8,128)}) custom-call(f32[16,32,128]{2,1,0:T(8,128)} %b_ref.1, f32[16,32,128]{2,1,0:T(8,128)} %c_ref.1, f32[8,8,128]{2,1,0:T(8,128)} %constant.14.clone.rest_0_, f32[256,256]{1,0:T(8,128)} %constant.15.clone.rest_1_, f32[256,256]{1,0:T(8,128)} %constant.16.clone.rest_2_, ...), custom_call_target="tpu_custom_call" | custom-call | tf_op jit(solution)/shard_map/pallas_call | solution.py:838
  70.2 1.8 %shard_map.105 = (f32[16,32,128]{2,1,0:T(8,128)}, f32[16,32,128]{2,1,0:T(8,128)}) custom-call(f32[16,32,128]{2,1,0:T(8,128)} %get-tuple-element.4.first, f32[16,32,128]{2,1,0:T(8,128)} %get-tuple-element.5.second), custom_call_target="tpu_custom_call" | custom-call | tf_op jit(solution)/shard_map/pallas_call | solution.py:838

commit v6 on v5

--- a/solution.py
+++ b/solution.py
@@ -107,7 +107,7 @@
             _, count, tall = self.part(o)
             self.slot[o] = at
             at += count
-            height[tall < 8] += count * tall
+            height[o[0] != 0] += count * tall
         self.received = at
         self.vectors = [h // 8 for h in height]
 
@@ -141,8 +141,13 @@
          red_xy, red_z, gsend, grecv, ssend, srecv, rsend, rrecv, load, fin) = rest
         gx, gy, gz = (lax.axis_index(a) for a in AXES)
 
+        steps = [
+            {0: at, 1: (at + 1) % size, -1: (at + size - 1) % size}
+            for at, size in ((gx, nx), (gy, ny), (gz, nz))
+        ]
+
         def near(o):
-            return ((gx + o[0] + nx) % nx, (gy + o[1] + ny) % ny, (gz + o[2] + nz) % nz)
+            return tuple(step[k] for step, k in zip(steps, o))
 
         def ring_xy(t):
             to = (gz // z_run + t // ny) % runs
@@ -234,7 +239,7 @@
                         src_ref=src.at[pl.ds(at, count), pl.ds(0, tall)],
                         dst_ref=dst.at[pl.ds(to, count), pl.ds(0, tall)],
                         send_sem=send_sem,
-                        recv_sem=recv_sem.at[1 if tall < 8 else 0],
+                        recv_sem=recv_sem.at[1 if o[0] else 0],
                         device_id=near(o),
                         device_id_type=MESH,
                     ).start()
@@ -329,11 +334,12 @@
             for k in range(n):
                 put(0, k, n, y_mask * jnp.where(ey >= 2, at((0, -1, 0), k), at((0, 1, 0), k)))
                 put(1, k, n, y_mask * unlane(low, high, k))
-                put(0, n, k, fx_lo * at((-1, 0, 0), k))
-                put(0, n + 1, k, fx_hi * at((1, 0, 0), k))
         def receive_far(dst, halo, sem, put):
             n = halo.n
             wait_halo(dst, halo, sem, 1)
+            for k in range(n):
+                put(0, n, k, fx_lo * dst[halo.slot[(-1, 0, 0)] + k])
+                put(0, n + 1, k, fx_hi * dst[halo.slot[(1, 0, 0)] + k])
             below = x_lanes(dst, halo, -1, -1), x_lanes(dst, halo, -1, 1)
             above = x_lanes(dst, halo, 1, -1), x_lanes(dst, halo, 1, 1)
             for k in range(n):

time: 72.1 us -> 72 us (level)
  no operation moved by 1% of the time
where the time goes in v6:
time: 72 us; the launch traced here: 71.8 us
  Pallas kernels  71.2 us (99%)
    pallas_call x2, Pallas kernels, shards(): return tuple(results(*call(right_side, coefficient, *tables)))  71.2 us

profile of v6, /device:TPU:1, one launch (start us, length us, event | category | flops | bytes accessed | tf_op | source)
XLA Modules:
  0.0 71.8 jit_solution(18276121454809638463)
XLA Ops:
  0.6 69.3 %shard_map.104 = (f32[16,32,128]{2,1,0:T(8,128)}, f32[16,32,128]{2,1,0:T(8,128)}) custom-call(f32[16,32,128]{2,1,0:T(8,128)} %b_ref.1, f32[16,32,128]{2,1,0:T(8,128)} %c_ref.1, f32[8,8,128]{2,1,0:T(8,128)} %constant.14.clone.rest_0_, f32[256,256]{1,0:T(8,128)} %constant.15.clone.rest_1_, f32[256,256]{1,0:T(8,128)} %constant.16.clone.rest_2_, ...), custom_call_target="tpu_custom_call" | custom-call | tf_op jit(solution)/shard_map/pallas_call | solution.py:844
  70.0 1.8 %shard_map.105 = (f32[16,32,128]{2,1,0:T(8,128)}, f32[16,32,128]{2,1,0:T(8,128)}) custom-call(f32[16,32,128]{2,1,0:T(8,128)} %get-tuple-element.4.first, f32[16,32,128]{2,1,0:T(8,128)} %get-tuple-element.5.second), custom_call_target="tpu_custom_call" | custom-call | tf_op jit(solution)/shard_map/pallas_call | solution.py:844
